TPU v7x, 512 devices: a whole 4x8x8 slice. The times are simulated.
512 devices in a mesh: emb: 128 (over z, y, core), dp: 4 (over x).
Axes of the slice: x: 4, y: 8, z: 8, core: 2. Of those that a mesh axis runs over, the one named last changes fastest.
Arguments:
- table_rows: bfloat16 [262144, 128], P(('emb', 'dp')), may hold values from -0.359375 to 0.359375
- piece_ids: int32 [2555904, 4], P(('emb', 'dp')), may hold values from 0 to 511
- piece_counts: int32 [2555904], P(('emb', 'dp')), may hold values from 1 to 4
- piece_dest: int32 [2555904, 1], P(('emb', 'dp')), may hold values from 0 to 127, as said below
- piece_target: int32 [2555904], P(('emb', 'dp')), may hold values from 0 to 3327, as said below
- labels: int32 [65536], P(('emb', 'dp')), may hold values 0 or 1
- w_first: bfloat16 [3328, 1024], P('emb'), may hold values from -0.8984375 to 0.8984375
- w_second: bfloat16 [1024, 512], replicated, may hold values from -0.1875 to 0.1875
- w_third: bfloat16 [512, 256], replicated, may hold values from -0.25 to 0.25
- w_out: bfloat16 [256], replicated, may hold values from -0.375 to 0.375
Outputs:
- row_grad: float32 [262144, 128], P(('emb', 'dp'))
- grad_second: float32 [1024, 512], replicated
- grad_third: float32 [512, 256], replicated
- grad_out: float32 [256], replicated
Inputs may be any that keep to these rules, and one draw needn't show every extreme that they name: `piece_dest`: at most 78 pieces of one device's block name the same destination, and every block has exactly 78 for one destination. `piece_target`: every bag of every sample block has at least one piece.
All inputs are finite; a program needn't handle non-finite values. No bound on the sum of `labels` on one device may be relied on, other than what follows from the above.
Results may differ from a plain program's by a relative error of at most 0.006.
Values may be sent and summed in bfloat16 or wider, within the bound.
A program may use at most 128 MiB of HBM per device.

v0:
```python
import jax
import jax.numpy as jnp
from jax import lax
from jax.sharding import PartitionSpec as P

FIELDS = 26


coef = 0.7978845608028654


def act_slope(values):
    inner = coef * (values + 0.044715 * values * values * values)
    tangent = jnp.tanh(inner)
    result = 0.5 * values * (1.0 + tangent)
    slope = 0.5 * (1.0 + tangent) + 0.5 * values * (1.0 - tangent * tangent) * coef * (
        1.0 + 3.0 * 0.044715 * values * values
    )
    return (result, slope)


def contract_last(left, right):
    return lax.dot_general(
        left, right, (((1,), (1,)), ((), ())), preferred_element_type=jnp.float32
    )


def contract_first(left, right):
    return lax.dot_general(
        left, right, (((0,), (0,)), ((), ())), preferred_element_type=jnp.float32
    )


def per_device(
    table_rows,
    piece_ids,
    piece_counts,
    piece_dest,
    piece_target,
    labels,
    w_first,
    w_second,
    w_third,
    w_out,
):
    shards = lax.axis_size("emb")
    pieces = piece_ids.shape[0]
    width_ids = piece_ids.shape[1]
    touched = table_rows.shape[0]
    emb_width = table_rows.shape[1]
    samples = labels.shape[0]
    capacity = 2 * pieces // shards
    live_ids = jnp.arange(width_ids)[None, :] < piece_counts[:, None]
    summed = jnp.zeros((pieces, emb_width), jnp.float32)
    for column in range(width_ids):
        picked = table_rows[piece_ids[:, column]]
        summed = summed + jnp.where(
            live_ids[:, column : column + 1], picked, jnp.zeros_like(picked)
        ).astype(jnp.float32)
    pooled = summed.astype(jnp.bfloat16)
    target_shard = piece_dest[:, 0]
    member = (target_shard[:, None] == jnp.arange(shards)[None, :]).astype(jnp.int32)
    earlier = jnp.cumsum(member, axis=0) - member
    slot_rank = jnp.sum(earlier * member, axis=1)
    slot_index = target_shard * capacity + slot_rank
    outgoing = jnp.zeros((shards * capacity, emb_width), jnp.bfloat16).at[slot_index].set(pooled)
    slot_owner = jnp.zeros((shards * capacity,), jnp.int32).at[slot_index].set(piece_target + 1)
    arrived, arrived_owner = (
        lax.all_to_all(
            outgoing.reshape(shards, capacity, emb_width),
            "emb",
            split_axis=0,
            concat_axis=0,
            tiled=True,
        ),
        lax.all_to_all(
            slot_owner.reshape(shards, capacity), "emb", split_axis=0, concat_axis=0, tiled=True
        ),
    )
    flat_owner = arrived_owner.reshape(-1)
    bags = jax.ops.segment_sum(
        arrived.reshape(-1, emb_width).astype(jnp.float32),
        flat_owner,
        num_segments=samples * FIELDS + 1,
    )[1:]
    features = bags.astype(jnp.bfloat16).reshape(samples, FIELDS * emb_width)
    truth = labels.astype(jnp.float32)
    gathered = lax.all_gather(w_first, "emb", axis=0, tiled=True)
    first_pre = jnp.dot(features, gathered, preferred_element_type=jnp.float32)
    first_act, first_slope = act_slope(first_pre)
    first_act = first_act.astype(jnp.bfloat16)
    second_act, second_slope = act_slope(
        jnp.dot(first_act, w_second, preferred_element_type=jnp.float32)
    )
    second_act = second_act.astype(jnp.bfloat16)
    third_act, third_slope = act_slope(
        jnp.dot(second_act, w_third, preferred_element_type=jnp.float32)
    )
    third_act = third_act.astype(jnp.bfloat16)
    deep = jnp.dot(third_act, w_out, preferred_element_type=jnp.float32)
    vectors = features.reshape(samples, FIELDS, emb_width).astype(jnp.float32)
    total = jnp.sum(vectors, axis=1)
    pairs = 0.5 * jnp.sum(total * total - jnp.sum(vectors * vectors, axis=1), axis=1)
    logit_grad = jax.nn.sigmoid(deep + pairs) - truth
    grad_out = jnp.sum(logit_grad[:, None] * third_act.astype(jnp.float32), axis=0)
    third_grad = (logit_grad[:, None] * w_out.astype(jnp.float32)[None, :] * third_slope).astype(
        jnp.bfloat16
    )
    grad_third = contract_first(second_act, third_grad)
    second_grad = (contract_last(third_grad, w_third) * second_slope).astype(jnp.bfloat16)
    grad_second = contract_first(first_act, second_grad)
    first_grad = (contract_last(second_grad, w_second) * first_slope).astype(jnp.bfloat16)
    network = contract_last(first_grad, gathered)
    network = network.reshape(samples, FIELDS, emb_width)
    feature_grad = (network + logit_grad[:, None, None] * (total[:, None, :] - vectors)).astype(
        jnp.bfloat16
    )
    padded = jnp.concatenate(
        [jnp.zeros((1, emb_width), jnp.bfloat16), feature_grad.reshape(-1, emb_width)], axis=0
    )
    returned = padded[flat_owner].reshape(shards, capacity, emb_width)
    came_back = lax.all_to_all(returned, "emb", split_axis=0, concat_axis=0, tiled=True)
    piece_grad = came_back.reshape(-1, emb_width)[slot_index]
    row_grad = jnp.zeros((touched, emb_width), jnp.float32)
    for column in range(width_ids):
        chosen = jnp.where(
            live_ids[:, column : column + 1], piece_grad, jnp.zeros((), jnp.bfloat16)
        )
        row_grad = row_grad + jax.ops.segment_sum(
            chosen.astype(jnp.float32), piece_ids[:, column], num_segments=touched
        )
    grad_second, grad_third, grad_out = lax.psum((grad_second, grad_third, grad_out), ("emb", "dp"))
    return (row_grad, grad_second, grad_third, grad_out)


def solution(mesh):
    in_specs = (
        P(("emb", "dp"), None),
        P(("emb", "dp"), None),
        P(("emb", "dp")),
        P(("emb", "dp"), None),
        P(("emb", "dp")),
        P(("emb", "dp")),
        P("emb", None),
        P(),
        P(),
        P(),
    )
    out_specs = (P(("emb", "dp"), None), P(), P(), P())
    return jax.shard_map(
        per_device, mesh=mesh, in_specs=in_specs, out_specs=out_specs, check_vma=False
    )
```

profile of v0, /device:TPU:1, one launch (start us, length us, event | category | flops | bytes accessed | tf_op | source)
XLA Modules:
  0.0 697.9 jit_solution(1595075859405786613)
XLA Ops:
  9.6 1.6 copy-done.2
  11.2 1.9 broadcast_add_fusion
  13.7 3.1 fusion.3
  16.9 24.1 %scatter_custom_fusion = s32[9984]{0:T(1024)S(1)} fusion(s32[4992]{0:T(1024)S(1)} %fusion.84, s32[4992]{0:T(1024)S(1)} %broadcast_add_fusion.1, s32[]{:T(128)} %constant.15.clone.1), kind=kCustom, calls=%fused_computation.133 | custom fusion | bytes 39940 | tf_op jit(solution)/shard_map/scatter | solution.py:67
  41.7 19.1 %all-to-all-start = ((s32[128,1,78]{2,1,0:T(1,128)}), s32[128,1,78]{2,1,0:T(1,128)S(1)}, u32[]{:S(2)}, u32[]{:S(2)}) async-start(s32[128,1,78]{2,1,0:T(1,128)} %bitcast.3), calls=%async_computation | async-start | bytes 131072 | tf_op jit(solution)/shard_map/all_to_all | solution.py:76
  62.2 86.9 %scatter_custom_fusion.1 = bf16[9984,128]{1,0:T(8,128)(2,1)} fusion(s32[4992]{0:T(1024)S(1)} %fusion.84, bf16[]{:T(256)} %constant.19.clone.1, pred[4992]{0:T(1024)(128)(4,1)S(1)} %get-tuple-element.15, pred[4992]{0:T(1024)(128)(4,1)S(1)} %get-tuple-element.16, pred[4992]{0:T(1024)(128)(4,1)S(1)} %get-tuple-element.17, ...), kind=kCustom, calls=%fused_computation.34 | custom fusion | flops 7667712 | bytes 3183616 | tf_op jit(solution)/shard_map/scatter | solution.py:66
  149.1 4.9 reshape.90
  154.0 14.1 %all-to-all-start.1 = ((bf16[128,78,128]{2,1,0:T(8,128)(2,1)}), bf16[128,78,128]{2,1,0:T(8,128)(2,1)}, u32[]{:S(2)}, u32[]{:S(2)}) async-start(bf16[128,78,128]{2,1,0:T(8,128)(2,1)} %reshape.90), calls=%async_computation.1 | async-start | bytes 5242880 | tf_op jit(solution)/shard_map/all_to_all | solution.py:69
  170.5 59.2 %all-to-all-done.1 = bf16[128,78,128]{2,1,0:T(8,128)(2,1)} async-done(((bf16[128,78,128]{2,1,0:T(8,128)(2,1)}), bf16[128,78,128]{2,1,0:T(8,128)(2,1)}, u32[]{:S(2)}, u32[]{:S(2)}) %all-to-all-start.1) | async-done | bytes 2555936 | tf_op jit(solution)/shard_map/all_to_all | solution.py:69
  229.7 5.1 reshape.165
  234.8 61.2 %scatter_custom_fusion.2 = f32[3329,128]{1,0:T(8,128)} fusion(s32[9984]{0:T(1024)S(1)} %reshape.163, f32[9984,128]{1,0:T(8,128)} %reshape.165, f32[]{:T(128)} %constant.13.clone.1), kind=kCustom, calls=%fused_computation.64 | custom fusion | flops 1277952 | bytes 1704960 | tf_op jit(solution)/shard_map/scatter-add | solution.py:81
  296.0 1.6 slice.102
  298.6 1.9 reshape.91
  302.8 1.3 sub.36
  304.2 10.4 %reshape.203 = bf16[3328,1024]{1,0:T(8,128)(2,1)} reshape(bf16[128,26,1024]{2,1,0:T(8,128)(2,1)} %all-gather.3.cloned.1.call-done) | data formatting | bytes 13631488
  314.6 4.0 fusion.105
  320.3 5.3 fusion.33
  325.6 1.3 reshape.92
  326.9 3.0 add_convert_fusion.1
  330.1 20.8 %gather_fusion = bf16[9984,128]{1,0:T(8,128)(2,1)} fusion(bf16[3329,128]{1,0:T(8,128)(2,1)S(1)} %concatenate.3, s32[10240]{0:T(1024)S(1)} %pad_clamp_fusion), kind=kCustom, calls=%fused_computation.4 | custom fusion | bytes 5151744 | tf_op jit(solution)/shard_map/gather | solution.py:121
  350.9 4.9 reshape.93
  355.8 10.2 %all-to-all-start.2 = ((bf16[128,78,128]{2,1,0:T(8,128)(2,1)}), bf16[128,78,128]{2,1,0:T(8,128)(2,1)}, u32[]{:S(2)}, u32[]{:S(2)}) async-start(bf16[128,78,128]{2,1,0:T(8,128)(2,1)} %reshape.93), calls=%async_computation.2 | async-start | bytes 5242880 | tf_op jit(solution)/shard_map/all_to_all | solution.py:122
  367.3 1.8 fusion.100
  369.2 146.2 %psum.23 = f32[256]{0:T(256)} all-reduce(f32[256]{0:T(256)S(1)} %multiply_reduce_fusion.1), channel_id=1, replica_groups=mesh['emb'=128,'dp'=4] {'emb','dp'}, use_global_device_ids=true, to_apply=%region_16.17 | all-reduce | flops 256 | bytes 2048 | tf_op jit(solution)/shard_map/psum | solution.py:132
  515.4 4.9 reshape.94
  520.4 10.5 %gather_fusion.1 = bf16[4992,128]{1,0:T(8,128)(2,1)S(1)} fusion(bf16[9984,128]{1,0:T(8,128)(2,1)} %reshape.94, s32[5120]{0:T(1024)S(1)} %pad_clamp_fusion.1), kind=kCustom, calls=%fused_computation.5 | custom fusion | bytes 2575872 | tf_op jit(solution)/shard_map/gather | solution.py:123
  530.9 31.0 %scatter_custom_fusion.4 = f32[512,128]{1,0:T(8,128)S(1)} fusion(s32[4992]{0:T(1024)} %get-tuple-element.11, bf16[4992,128]{1,0:T(8,128)(2,1)S(1)} %gather_fusion.1, pred[4992]{0:T(1024)(128)(4,1)S(1)} %copy-done.16, bf16[]{:T(256)} %constant.19.clone.1, f32[]{:T(128)} %constant.13.clone.1), kind=kCustom, calls=%fused_computation.23 | custom fusion | flops 1916928 | bytes 1546112 | tf_op jit(solution)/shard_map/scatter-add | solution.py:129
  562.0 31.0 %scatter_custom_fusion.3 = f32[512,128]{1,0:T(8,128)S(1)} fusion(s32[4992]{0:T(1024)} %get-tuple-element.12, bf16[4992,128]{1,0:T(8,128)(2,1)S(1)} %gather_fusion.1, pred[4992]{0:T(1024)(128)(4,1)S(1)} %copy-done.14, bf16[]{:T(256)} %constant.19.clone.1, f32[]{:T(128)} %constant.13.clone.1), kind=kCustom, calls=%fused_computation.25 | custom fusion | flops 1916928 | bytes 1546112 | tf_op jit(solution)/shard_map/scatter-add | solution.py:129
  593.0 31.0 %scatter_custom_fusion.6 = f32[512,128]{1,0:T(8,128)S(1)} fusion(s32[4992]{0:T(1024)} %get-tuple-element.6, bf16[4992,128]{1,0:T(8,128)(2,1)S(1)} %gather_fusion.1, pred[4992]{0:T(1024)(128)(4,1)S(1)} %copy-done.12, bf16[]{:T(256)} %constant.19.clone.1, f32[]{:T(128)} %constant.13.clone.1), kind=kCustom, calls=%fused_computation.19 | custom fusion | flops 1916928 | bytes 1546112 | tf_op jit(solution)/shard_map/scatter-add | solution.py:129
  624.1 31.3 %scatter_custom_fusion.5 = f32[512,128]{1,0:T(8,128)S(1)} fusion(f32[512,128]{1,0:T(8,128)S(1)} %add.157, s32[4992]{0:T(1024)} %get-tuple-element.13, bf16[4992,128]{1,0:T(8,128)(2,1)S(1)} %gather_fusion.1, pred[4992]{0:T(1024)(128)(4,1)S(1)} %copy-done.10, bf16[]{:T(256)} %constant.19.clone.1), kind=kCustom, calls=%fused_computation.21 | custom fusion | flops 1916928 | bytes 1545728 | tf_op jit(solution)/shard_map/scatter-add | solution.py:129
  656.1 30.7 %all-reduce.4.cloned.1.call-done = (f32[1024,512]{1,0:T(8,128)}, f32[512,256]{1,0:T(8,128)}) async-done(((f32[1024,512]{1,0:T(8,128)}, f32[512,256]{1,0:T(8,128)}), (f32[1024,512]{1,0:T(8,128)}, f32[512,256]{1,0:T(8,128)})) %all-reduce.4.cloned.1.call-update) | async-done | bytes 2621456 | tf_op jit(solution)/shard_map/psum | solution.py:132
  686.8 3.2 copy.23
  (101 shorter events, 15.6 us)
Async XLA Ops:
  7.2 311.5 %copy-start = (bf16[1024,512]{1,0:T(8,128)(2,1)S(1)}, bf16[1024,512]{1,0:T(8,128)(2,1)}, u32[]{:S(2)}) copy-start(bf16[1024,512]{1,0:T(8,128)(2,1)} %param.17) | copy-start | bytes 3145732
  7.2 297.0 %all-gather.3.cloned.1.call-start = ((), (), s32[]{:S(2)}) async-start(), calls=%async_computation.3 | async-start | bytes 8454144 | tf_op jit(solution)/shard_map/all_gather | solution.py:88
  9.5 1.6 copy-start.2
  13.6 3.1 copy-start.7
  13.6 3.2 copy-start.17
  13.6 47.1 %copy-start.8 = (s32[4992,4]{0,1:T(4,128)S(1)}, s32[4992,4]{0,1:T(4,128)}, u32[]{:S(2)}) copy-start(s32[4992,4]{0,1:T(4,128)} %param.11) | copy-start | bytes 239620
  13.6 48.2 %copy-start.18 = (s32[4992]{0:T(1024)S(1)}, s32[4992]{0:T(1024)}, u32[]{:S(2)}) copy-start(s32[4992]{0:T(1024)} %param.12) | copy-start | bytes 59908
  13.7 48.5 %copy-start.5 = (bf16[512,128]{1,0:T(8,128)(2,1)S(1)}, bf16[512,128]{1,0:T(8,128)(2,1)}, u32[]{:S(2)}) copy-start(bf16[512,128]{1,0:T(8,128)(2,1)} %param.10) | copy-start | bytes 393220
  41.7 112.3 %all-to-all-start = ((s32[128,1,78]{2,1,0:T(1,128)}), s32[128,1,78]{2,1,0:T(1,128)S(1)}, u32[]{:S(2)}, u32[]{:S(2)}) async-start(s32[128,1,78]{2,1,0:T(1,128)} %bitcast.3), calls=%async_computation | async-start | bytes 131072 | tf_op jit(solution)/shard_map/all_to_all | solution.py:76
  62.1 91.8 %copy-start.9 = (pred[4992]{0:T(1024)(128)(4,1)}, pred[4992]{0:T(1024)(128)(4,1)S(1)}, u32[]{:S(2)}) copy-start(pred[4992]{0:T(1024)(128)(4,1)S(1)} %get-tuple-element.16) | copy-start | bytes 14980
  62.2 91.8 %copy-start.11 = (pred[4992]{0:T(1024)(128)(4,1)}, pred[4992]{0:T(1024)(128)(4,1)S(1)}, u32[]{:S(2)}) copy-start(pred[4992]{0:T(1024)(128)(4,1)S(1)} %get-tuple-element.15) | copy-start | bytes 14980
  62.2 91.8 %copy-start.13 = (pred[4992]{0:T(1024)(128)(4,1)}, pred[4992]{0:T(1024)(128)(4,1)S(1)}, u32[]{:S(2)}) copy-start(pred[4992]{0:T(1024)(128)(4,1)S(1)} %get-tuple-element.14) | copy-start | bytes 14980
  62.2 91.8 %copy-start.15 = (pred[4992]{0:T(1024)(128)(4,1)}, pred[4992]{0:T(1024)(128)(4,1)S(1)}, u32[]{:S(2)}) copy-start(pred[4992]{0:T(1024)(128)(4,1)S(1)} %get-tuple-element.17) | copy-start | bytes 14980
  154.0 14.2 %copy-start.20 = (bf16[256]{0:T(256)(128)(2,1)S(1)}, bf16[256]{0:T(256)(128)(2,1)}, u32[]{:S(2)}) copy-start(bf16[256]{0:T(256)(128)(2,1)} %param.19) | copy-start | bytes 1540
  154.0 75.7 %all-to-all-start.1 = ((bf16[128,78,128]{2,1,0:T(8,128)(2,1)}), bf16[128,78,128]{2,1,0:T(8,128)(2,1)}, u32[]{:S(2)}, u32[]{:S(2)}) async-start(bf16[128,78,128]{2,1,0:T(8,128)(2,1)} %reshape.90), calls=%async_computation.1 | async-start | bytes 5242880 | tf_op jit(solution)/shard_map/all_to_all | solution.py:69
  297.6 1.0 copy-start.3
  304.2 10.4 %copy-start.4 = (bf16[128,3328]{1,0:T(8,128)(2,1)S(1)}, bf16[128,3328]{1,0:T(8,128)(2,1)}, u32[]{:S(2)}) copy-start(bf16[128,3328]{1,0:T(8,128)(2,1)} %reshape.91) | copy-start | bytes 2555908
  314.6 4.4 copy-start.19
  318.7 0.7 copy-start.21
  318.7 1.3 copy-start.22
  319.0 0.7 copy-start.24
  355.8 10.3 %copy-start.23 = (f32[256]{0:T(256)S(1)}, f32[256]{0:T(256)}, u32[]{:S(2)}) copy-start(f32[256]{0:T(256)} %convert_element_type.96) | copy-start | bytes 3076
  355.8 10.3 %copy-start.25 = (f32[128,512]{1,0:T(8,128)S(1)}, f32[128,512]{1,0:T(8,128)}, u32[]{:S(2)}) copy-start(f32[128,512]{1,0:T(8,128)} %copy-done.24) | copy-start | bytes 786436
  355.8 10.3 %copy-start.27 = (f32[128,256]{1,0:T(8,128)S(1)}, f32[128,256]{1,0:T(8,128)}, u32[]{:S(2)}) copy-start(f32[128,256]{1,0:T(8,128)} %copy-done.26) | copy-start | bytes 393220
  355.8 159.6 %all-to-all-start.2 = ((bf16[128,78,128]{2,1,0:T(8,128)(2,1)}), bf16[128,78,128]{2,1,0:T(8,128)(2,1)}, u32[]{:S(2)}, u32[]{:S(2)}) async-start(bf16[128,78,128]{2,1,0:T(8,128)(2,1)} %reshape.93), calls=%async_computation.2 | async-start | bytes 5242880 | tf_op jit(solution)/shard_map/all_to_all | solution.py:122
  366.0 320.8 %all-reduce.4.cloned.1.call-start = ((), (), s32[]{:S(2)}) async-start(), calls=%async_computation.4 | async-start | bytes 5242880 | tf_op jit(solution)/shard_map/psum | solution.py:132
  520.4 10.6 %copy-start.16 = (pred[4992]{0:T(1024)(128)(4,1)S(1)}, pred[4992]{0:T(1024)(128)(4,1)}, u32[]{:S(2)}) copy-start(pred[4992]{0:T(1024)(128)(4,1)} %copy-done.15) | copy-start | bytes 14980
  520.4 41.6 %copy-start.14 = (pred[4992]{0:T(1024)(128)(4,1)S(1)}, pred[4992]{0:T(1024)(128)(4,1)}, u32[]{:S(2)}) copy-start(pred[4992]{0:T(1024)(128)(4,1)} %copy-done.13) | copy-start | bytes 14980
  530.9 62.1 %copy-start.12 = (pred[4992]{0:T(1024)(128)(4,1)S(1)}, pred[4992]{0:T(1024)(128)(4,1)}, u32[]{:S(2)}) copy-start(pred[4992]{0:T(1024)(128)(4,1)} %copy-done.11) | copy-start | bytes 14980
  530.9 93.1 %copy-start.10 = (pred[4992]{0:T(1024)(128)(4,1)S(1)}, pred[4992]{0:T(1024)(128)(4,1)}, u32[]{:S(2)}) copy-start(pred[4992]{0:T(1024)(128)(4,1)} %copy-done.9) | copy-start | bytes 14980
  686.8 3.2 copy-start.6
  686.8 4.0 copy-start.1
  (1 other events, 0.7 us)
Sparse Core Ops, SparseCore 0:
  11.1 94.0 all-gather.2
  372.3 314.4 all-reduce.3
where the time goes:
time: 705 us; the launch traced here: 698 us
  other arithmetic  287 us (41%)
  blocking collectives  146 us (21%)
  local copies, waits for them, and re-layouts  103 us (15%)
  waiting for transfers between devices  90.6 us (13%)
  starting transfers between devices  43.5 us (6%)
  between operations  14.9 us (2%)
  matrix products  13.3 us (2%)
    psum x1, blocking collectives, per_device(): lax.psum((grad_second, grad_third, grad_out), ('emb', 'dp'))  146 us
    scatter-add x4, other arithmetic, per_device(): jax.ops.segment_sum(chosen.astype(jnp.float32), piece_ids[:, column], num...  124 us
    scatter x1, other arithmetic, per_device(): jnp.zeros((shards * capacity, emb_width), jnp.bfloat16).at[slot_index]  86.9 us
    scatter-add x1, other arithmetic, per_device(): jax.ops.segment_sum(arrived.reshape(-1, emb_width).astype(jnp.float32), f...  61.2 us
    all_to_all x1, waiting for transfers between devices, per_device(): lax.all_to_all(outgoing.reshape(shards, capacity, emb_width), 'emb', spli...  59.2 us
    psum x1, waiting for transfers between devices, per_device(): lax.psum((grad_second, grad_third, grad_out), ('emb', 'dp'))  30.7 us
    scatter x1, local copies, waits for them, and re-layouts, per_device(): jnp.zeros((shards * capacity,), jnp.int32).at[slot_index]  24.1 us
    gather x1, local copies, waits for them, and re-layouts, per_device(): returned = padded[flat_owner].reshape(shards, capacity, emb_width)  20.8 us
  transfers between devices with their start and end apart: 5, of which 2 were waited for; matrix products, arithmetic and copies ran while one was open for 49% of the time, Pallas kernels for 0%

commit v1 on v0

v1 whole, which is shorter than its diff:
```python
import jax
import jax.numpy as jnp
from jax import lax
from jax.experimental import pallas as pl
from jax.experimental.pallas import tpu as pltpu
from jax.sharding import PartitionSpec as P

FIELDS = 26
LANES = 128
CAP = 80
PIECE_CHUNK = 384
SHARD_ROWS = 26
PAD_ROWS = 32

BF = jnp.bfloat16
F32 = jnp.float32

coef = 0.7978845608028654


def act_slope(values):
    inner = coef * (values + 0.044715 * values * values * values)
    tangent = jnp.tanh(inner)
    result = 0.5 * values * (1.0 + tangent)
    slope = 0.5 * (1.0 + tangent) + 0.5 * values * (1.0 - tangent * tangent) * coef * (
        1.0 + 3.0 * 0.044715 * values * values
    )
    return (result, slope)


def contract(left, right, left_dim, right_dim):
    return lax.dot_general(
        left, right, (((left_dim,), (right_dim,)), ((), ())), preferred_element_type=F32
    )


def iota(shape, dim):
    return lax.broadcasted_iota(jnp.int32, shape, dim)


def one_hot(condition):
    return jnp.where(condition, 1.0, 0.0).astype(BF)


def slots_kernel(dest_ref, target_ref, count_ref, ids_ref, slots_ref):
    pieces = dest_ref.shape[1]
    shards = slots_ref.shape[1]
    chunk = PIECE_CHUNK
    before = one_hot(iota((chunk, chunk), 0) < iota((chunk, chunk), 1))
    carry = jnp.zeros((shards, 1), F32)
    total = None
    for step in range(pieces // chunk):
        part = slice(step * chunk, (step + 1) * chunk)
        is_dest = jnp.where(iota((shards, chunk), 0) == dest_ref[:, part], 1.0, 0.0)
        to_dest = is_dest.astype(BF)
        earlier = contract(to_dest, before, 1, 0) + carry
        rank = jnp.sum(is_dest * earlier, axis=0, keepdims=True)
        carry = carry + jnp.sum(is_dest, axis=1, keepdims=True)
        at_rank = one_hot(iota((LANES, chunk), 0).astype(F32) == rank)
        target = target_ref[:, part]
        sample = (target * 2521) // 65536
        field = target - sample * FIELDS
        count = count_ref[:, part]
        numbers = [field + 1, sample]
        for column in range(ids_ref.shape[0]):
            ids = ids_ref[column : column + 1, part]
            numbers.append(jnp.where(column < count, ids // LANES + 1, 0))
            numbers.append(ids % LANES)
        scaled = jnp.concatenate(
            [to_dest * number.astype(F32).astype(BF) for number in numbers], axis=0
        )
        placed = contract(scaled, at_rank, 1, 1)
        total = placed if total is None else total + placed
    for column in range(slots_ref.shape[0]):
        slots_ref[column] = total[column * shards : (column + 1) * shards]


def count_rows(high, low, height):
    slots = low[0].shape[1]
    lows = [one_hot(iota((LANES, slots), 0).astype(F32) == row) for row in low]
    tiles = []
    for tile in range(height):
        parts = [one * one_hot(row == tile + 1.0) for one, row in zip(lows, high)]
        tiles.append((parts[0] + parts[1]) + (parts[2] + parts[3]))
    return jnp.concatenate(tiles, axis=0)


def number_rows(numbers_ref, shards):
    def row(column):
        return jnp.concatenate([numbers_ref[column, pl.ds(one, 1)] for one in shards], axis=1)

    return [row(2 + 2 * k) for k in range(4)], [row(3 + 2 * k) for k in range(4)]


STEPS = 32


def quad(step):
    flip = step % 2
    place = (step // 2 * 7 + 2) % 16
    a, b = 1 + place // 4, place % 4
    last = 4 * ((place // 12) * ((4 - b) // 4))
    return flip, place, ((a, b), (8 - b, a), (8 + last - a, 8 - b), (b + last, 8 - a))


def shard_at(flip, move, sign):
    emb = lax.axis_index("emb")
    z = (emb // 16 + 8 + sign * move[0]) % 8
    y = ((emb // 2) % 8 + 8 + sign * move[1]) % 8
    return z * 16 + y * 2 + (emb + flip) % 2


def greet_all():
    emb = lax.axis_index("emb")
    barrier = pltpu.get_barrier_semaphore()

    def greet(step, carry):
        pl.semaphore_signal(
            barrier,
            inc=1,
            device_id={"emb": (emb + step) % LANES},
            device_id_type=pl.DeviceIdType.MESH,
        )
        return carry

    lax.fori_loop(1, LANES, greet, 0)
    return barrier


def send_block(step, which, flip, place, shard, send_ref, recv_ref, send_sem, recv_sem):
    emb = lax.axis_index("emb")
    source = send_ref.at[shard]
    target = recv_ref.at[emb, pl.ds(0, CAP)]

    def away():
        send_to({"emb": shard}, source, target, send_sem, recv_sem.at[step])

    if which != 2:
        away()
        return
    own = (place == 12) & (flip == 0)

    @pl.when(own)
    def _():
        pltpu.make_async_copy(source, target, recv_sem.at[step]).start()

    @pl.when(jnp.logical_not(own))
    def _():
        away()


def forward_kernel(
    numbers_ref, rows_ref, out_ref, owners_ref, send_ref, recv_ref, sums_ref, send_sem, recv_sem
):
    shards = recv_ref.shape[0]
    recv_ref[:, CAP:] = jnp.zeros((shards, LANES - CAP, LANES), BF)
    pl.semaphore_wait(greet_all(), LANES - 1)

    def send(step, carry):
        flip, place, moves = quad(step)
        for which, move in enumerate(moves):
            shard = shard_at(flip, move, 1)
            high, low = number_rows(numbers_ref, [shard])
            counts = count_rows(high, low, rows_ref.shape[0] // LANES)
            pooled = contract(counts, rows_ref[...], 0, 0)[:CAP]
            end = iota((8, LANES), 0)
            tail = jnp.where(end == 6, numbers_ref[0, pl.ds(shard, 1)], pooled[CAP - 8 :])
            tail = jnp.where(end == 7, numbers_ref[1, pl.ds(shard, 1)], tail)
            send_ref[shard] = jnp.concatenate([pooled[: CAP - 8], tail], axis=0).astype(BF)
            send_block(step, which, flip, place, shard, send_ref, recv_ref, send_sem, recv_sem)
        return carry

    lax.fori_loop(0, STEPS, send, 0)
    sums_ref[...] = jnp.zeros_like(sums_ref)

    def receive(step, carry):
        flip, _, moves = quad(step)
        wait_for(send_ref.at[pl.ds(0, 4)], recv_sem.at[step])
        arrived, fields, samples = [], [], []
        for move in moves:
            shard = shard_at(flip, move, -1)
            block = recv_ref[shard]
            tail = block[CAP - 16 : CAP].astype(F32)
            arrived.append(block)
            fields.append(tail[14:15])
            samples.append(tail[15:16])
            owners_ref[0, pl.ds(shard, 1)] = fields[-1]
            owners_ref[1, pl.ds(shard, 1)] = samples[-1]
        arrived = jnp.concatenate(arrived, axis=0)
        field = jnp.concatenate(fields, axis=1)
        sample = jnp.concatenate(samples, axis=1)
        in_sample = one_hot(iota((LANES, 4 * LANES), 0).astype(F32) == sample)
        for tile in range(FIELDS):
            member = in_sample * one_hot(field == tile + 1.0)
            sums_ref[tile] += jnp.dot(member, arrived, preferred_element_type=F32)
        return carry

    lax.fori_loop(0, STEPS, receive, 0)
    wait_for(send_ref.at[pl.ds(0, LANES - 1)], send_sem)
    for tile in range(FIELDS):
        out_ref[:, tile * LANES : (tile + 1) * LANES] = sums_ref[tile].astype(BF)


def window_tile(tile):
    start = tile * 4 * SHARD_ROWS
    return min(start // LANES, FIELDS - 2), start


def window_map(tile):
    first, start = window_tile(tile)
    feature = iota((2 * LANES, LANES), 0) + (first * LANES - start)
    place = iota((2 * LANES, LANES), 1)
    row = place % PAD_ROWS
    wanted = (place // PAD_ROWS) * SHARD_ROWS + row
    return jnp.where(row < SHARD_ROWS, one_hot(feature == wanted), jnp.zeros((), BF))


def dense_kernel(
    feature_ref, label_ref, first_ref, second_ref, third_ref, last_ref,
    grad_ref, packed_ref, padded_ref, network_ref,
):
    padded_tiles = first_ref.shape[0] // LANES
    for tile in range(padded_tiles):
        first, _ = window_tile(tile)
        window = feature_ref[:, first * LANES : (first + 2) * LANES]
        padded = jnp.dot(window, window_map(tile), preferred_element_type=F32)
        padded_ref[:, tile * LANES : (tile + 1) * LANES] = padded.astype(BF)
    first_pre = jnp.dot(padded_ref[...], first_ref[...], preferred_element_type=F32)
    first_act, first_slope = act_slope(first_pre)
    first_act = first_act.astype(BF)
    second_act, second_slope = act_slope(
        jnp.dot(first_act, second_ref[...], preferred_element_type=F32)
    )
    second_act = second_act.astype(BF)
    third_act, third_slope = act_slope(
        jnp.dot(second_act, third_ref[...], preferred_element_type=F32)
    )
    third_act = third_act.astype(BF).astype(F32)
    last = last_ref[...].astype(F32)
    deep = jnp.sum(third_act * last, axis=1, keepdims=True)
    total = jnp.zeros((feature_ref.shape[0], LANES), F32)
    squares = jnp.zeros((feature_ref.shape[0], LANES), F32)
    for tile in range(FIELDS):
        vector = feature_ref[:, tile * LANES : (tile + 1) * LANES].astype(F32)
        total = total + vector
        squares = squares + vector * vector
    pairs = 0.5 * jnp.sum(total * total - squares, axis=1, keepdims=True)
    logit_grad = jax.nn.sigmoid(deep + pairs) - label_ref[...].astype(F32)
    h1, h2 = second_ref.shape
    h3 = third_ref.shape[1]
    start = h1 * h2 // LANES
    end = start + h2 * h3 // LANES
    packed_ref[end:] = jnp.zeros_like(packed_ref[end:])
    grad_out = jnp.sum(logit_grad * third_act, axis=0, keepdims=True)
    for tile in range(h3 // LANES):
        packed_ref[end + 8 * tile : end + 8 * tile + 1] = grad_out[
            :, tile * LANES : (tile + 1) * LANES
        ]
    third_grad = (logit_grad * last * third_slope).astype(BF)
    grad_third = contract(second_act, third_grad, 0, 0)
    for tile in range(h3 // LANES):
        packed_ref[start + tile * h2 : start + (tile + 1) * h2] = grad_third[
            :, tile * LANES : (tile + 1) * LANES
        ]
    second_grad = (contract(third_grad, third_ref[...], 1, 1) * second_slope).astype(BF)
    for tile in range(h2 // LANES):
        packed_ref[tile * h1 : (tile + 1) * h1] = contract(
            first_act, second_grad[:, tile * LANES : (tile + 1) * LANES], 0, 0
        )
    first_grad = (contract(second_grad, second_ref[...], 1, 1) * first_slope).astype(BF)
    network_ref[...] = jnp.zeros_like(network_ref)
    for tile in range(padded_tiles):
        first, _ = window_tile(tile)
        part = contract(first_grad, first_ref[tile * LANES : (tile + 1) * LANES], 1, 1)
        upper = part.astype(BF)
        lower = (part - upper.astype(F32)).astype(BF)
        place = window_map(tile)
        moved = contract(upper, place, 1, 1) + contract(lower, place, 1, 1)
        network_ref[first] += moved[:, :LANES]
        network_ref[first + 1] += moved[:, LANES:]
    for tile in range(FIELDS):
        vector = feature_ref[:, tile * LANES : (tile + 1) * LANES].astype(F32)
        grad_ref[tile * LANES : (tile + 1) * LANES] = (
            network_ref[tile] + logit_grad * (total - vector)
        ).astype(BF)


def device(**axes):
    emb, dp = lax.axis_index("emb"), lax.axis_index("dp")
    z, y, core = emb // 16, (emb // 2) % 8, emb % 2
    z, y, core = axes.get("z", z), axes.get("y", y), axes.get("core", core)
    return {"emb": z * 16 + y * 2 + core, "dp": axes.get("x", dp)}


def send_to(partner, source, target, send_sem, recv_sem):
    pltpu.make_async_remote_copy(
        source,
        target,
        send_sem,
        recv_sem,
        device_id=partner,
        device_id_type=pl.DeviceIdType.MESH,
    ).start()


def wait_for(block, sem):
    pltpu.make_async_copy(block, block, sem).wait()


def reduce_steps(
    packed_ref, outs, full_ref, from_core, from_x, from_z, from_y, sum_core, sum_x, sum_z,
    send_sem, recv_sem,
):
    emb, x = lax.axis_index("emb"), lax.axis_index("dp")
    z, y, core = emb // 16, (emb // 2) % 8, emb % 2
    other = device(core=1 - core)

    def over_core():
        send_to(other, packed_ref.at[1 - core], from_core, send_sem.at[0], recv_sem.at[0])

    def over_x():
        wait_for(from_core, recv_sem.at[0])
        for part in range(4):
            sum_core[part] = packed_ref[core, part] + from_core[part]
        for step in range(1, 4):
            to = (x + step) % 4
            send_to(device(x=to), sum_core.at[to], from_x.at[x], send_sem.at[1], recv_sem.at[1])
        from_x[x] = sum_core[x]

    def over_z():
        wait_for(from_x.at[pl.ds(0, 3)], recv_sem.at[1])
        for part in range(8):
            sum_x[part] = (from_x[0, part] + from_x[1, part]) + (
                from_x[2, part] + from_x[3, part]
            )
        for step in range(1, 8):
            to = (z + step) % 8
            send_to(device(z=to), sum_x.at[to], from_z.at[z], send_sem.at[2], recv_sem.at[2])
        from_z[z] = sum_x[z]

    def over_y():
        wait_for(from_z.at[pl.ds(0, 7)], recv_sem.at[2])
        sum_z[...] = jnp.sum(from_z[...], axis=0)
        for step in range(1, 8):
            to = (y + step) % 8
            send_to(device(y=to), sum_z, from_y.at[y], send_sem.at[3], recv_sem.at[3])
        from_y[y] = sum_z[...]

    def gather_z():
        wait_for(from_y.at[pl.ds(0, 7)], recv_sem.at[3])
        full_ref[core, x, z] = jnp.sum(from_y[...], axis=0)
        mine = full_ref.at[core, x, z]
        for step in range(1, 8):
            send_to(device(z=(z + step) % 8), mine, mine, send_sem.at[4], recv_sem.at[4])

    def gather_x():
        wait_for(full_ref.at[core, x, pl.ds(0, 7)], recv_sem.at[4])
        mine = full_ref.at[core, x]
        for step in range(1, 4):
            send_to(device(x=(x + step) % 4), mine, mine, send_sem.at[5], recv_sem.at[5])

    def gather_core():
        wait_for(full_ref.at[core, pl.ds(0, 3)], recv_sem.at[5])
        mine = full_ref.at[core]
        send_to(other, mine, mine, send_sem.at[6], recv_sem.at[6])

    def finish():
        wait_for(full_ref.at[0], recv_sem.at[6])
        wait_for(from_core, send_sem.at[0])
        wait_for(from_x.at[pl.ds(0, 3)], send_sem.at[1])
        wait_for(from_z.at[pl.ds(0, 7)], send_sem.at[2])
        wait_for(from_y.at[pl.ds(0, 7)], send_sem.at[3])
        wait_for(full_ref.at[core, x, pl.ds(0, 7)], send_sem.at[4])
        wait_for(full_ref.at[core, pl.ds(0, 3)], send_sem.at[5])
        wait_for(full_ref.at[0], send_sem.at[6])
        for place, ref, column, row in grad_places(*outs):
            half, place = divmod(place, 4 * 8 * GRAD_ROWS)
            quarter, place = divmod(place, 8 * GRAD_ROWS)
            part, inside = divmod(place, GRAD_ROWS)
            ref[row : row + 8, column : column + LANES] = full_ref[
                half, quarter, part, inside : inside + 8
            ]

    return [over_core, over_x, over_z, over_y, gather_z, gather_x, gather_core, finish]


GRAD_ROWS = 88


def grad_places(second_ref, third_ref, out_ref):
    place = 0
    for ref in (second_ref, third_ref, out_ref):
        for column in range(0, ref.shape[1], LANES):
            for row in range(0, ref.shape[0], 8):
                yield place, ref, column, row
                place += 8


def backward_kernel(
    numbers_ref, owners_ref, grad_ref, packed_ref, out_ref, second_ref, third_ref, last_ref,
    send_ref, recv_ref, send_sem, recv_sem, *reduce_refs,
):
    x, shards = lax.axis_index("dp"), recv_ref.shape[0]
    recv_ref[:, CAP:] = jnp.zeros((shards, LANES - CAP, LANES), BF)
    out_ref[...] = jnp.zeros_like(out_ref)
    barrier = greet_all()
    for step in range(1, 4):
        pl.semaphore_signal(
            barrier,
            inc=1,
            device_id=device(x=(x + step) % 4),
            device_id_type=pl.DeviceIdType.MESH,
        )
    pl.semaphore_wait(barrier, LANES - 1 + 3)
    reduce = reduce_steps(packed_ref, (second_ref, third_ref, last_ref), *reduce_refs)

    def send(step, carry):
        flip, place, moves = quad(step)
        partners = [shard_at(flip, move, 1) for move in moves]
        members = []
        for shard in partners:
            square = (LANES, LANES)
            field = jnp.broadcast_to(owners_ref[0, pl.ds(shard, 1)], square).T[:CAP].astype(BF)
            sample = jnp.broadcast_to(owners_ref[1, pl.ds(shard, 1)], square).T[:CAP]
            in_sample = one_hot(iota((CAP, LANES), 1).astype(F32) == sample)
            none = jnp.zeros_like(in_sample)
            members.append(
                jnp.concatenate(
                    [
                        jnp.where(field == jnp.array(tile + 1.0, BF), in_sample, none)
                        for tile in range(FIELDS)
                    ],
                    axis=1,
                )
            )
        members = jnp.concatenate(members, axis=0)
        spread = jnp.dot(members, grad_ref[...], preferred_element_type=F32).astype(BF)
        for which, shard in enumerate(partners):
            send_ref[shard] = spread[which * CAP : (which + 1) * CAP]
            send_block(step, which, flip, place, shard, send_ref, recv_ref, send_sem, recv_sem)
        return carry

    def receive(step, carry):
        flip, _, moves = quad(step)
        wait_for(send_ref.at[pl.ds(0, 4)], recv_sem.at[step])
        partners = [shard_at(flip, move, -1) for move in moves]
        arrived = jnp.concatenate([recv_ref[shard] for shard in partners], axis=0)
        high, low = number_rows(numbers_ref, partners)
        counts = count_rows(high, low, out_ref.shape[0] // LANES)
        out_ref[...] += jnp.dot(counts, arrived, preferred_element_type=F32)
        return carry

    reduce[0]()
    lax.fori_loop(0, 8, send, 0)
    reduce[1]()
    lax.fori_loop(8, STEPS, send, 0)
    for part, reduce_step in enumerate(reduce[2:6]):
        reduce_step()
        lax.fori_loop(part * 8, part * 8 + 8, receive, 0)
    for reduce_step in reduce[6:]:
        reduce_step()
    wait_for(send_ref.at[pl.ds(0, LANES - 1)], send_sem)


PARAMS = pltpu.CompilerParams(vmem_limit_bytes=48 << 20)


def remote_params(collective_id):
    return pltpu.CompilerParams(
        vmem_limit_bytes=48 << 20, collective_id=collective_id, has_side_effects=True
    )


WHOLE = pl.BlockSpec(memory_space=pltpu.VMEM)


def cost(flops, bytes_accessed):
    return pl.CostEstimate(flops=flops, bytes_accessed=bytes_accessed, transcendentals=0)


def per_device(
    table_rows,
    piece_ids,
    piece_counts,
    piece_dest,
    piece_target,
    labels,
    w_first,
    w_second,
    w_third,
    w_out,
):
    shards = lax.axis_size("emb")
    pieces = piece_ids.shape[0]
    touched, width = table_rows.shape
    samples = labels.shape[0]
    h1, h2 = w_second.shape
    h3 = w_third.shape[1]
    slots = shards * CAP

    gathered = lax.all_gather(
        jnp.pad(w_first, ((0, PAD_ROWS - SHARD_ROWS), (0, 0))), "emb", axis=0, tiled=True
    )
    numbers = pl.pallas_call(
        slots_kernel,
        out_shape=jax.ShapeDtypeStruct((10, shards, LANES), F32),
        in_specs=[WHOLE] * 4,
        out_specs=WHOLE,
        compiler_params=PARAMS,
        cost_estimate=cost(2 * 1664 * pieces * LANES, 2_000_000),
    )(
        piece_dest.reshape(1, pieces),
        piece_target.reshape(1, pieces),
        piece_counts.reshape(1, pieces),
        piece_ids.T,
    )
    exchange = [
        pltpu.VMEM((shards, CAP, width), BF),
        pltpu.VMEM((shards, LANES, width), BF),
    ]
    features, owners = pl.pallas_call(
        forward_kernel,
        out_shape=(
            jax.ShapeDtypeStruct((samples, FIELDS * width), BF),
            jax.ShapeDtypeStruct((2, shards, LANES), F32),
        ),
        in_specs=[WHOLE] * 2,
        out_specs=(WHOLE,) * 2,
        scratch_shapes=exchange
        + [
            pltpu.VMEM((FIELDS, samples, width), F32),
            pltpu.SemaphoreType.DMA,
            pltpu.SemaphoreType.DMA((STEPS,)),
        ],
        compiler_params=remote_params(0),
        cost_estimate=cost(2 * slots * FIELDS * samples * width, 200_000_000),
    )(numbers, table_rows)
    feature_grad, packed = pl.pallas_call(
        dense_kernel,
        out_shape=(
            jax.ShapeDtypeStruct((FIELDS * samples, width), BF),
            jax.ShapeDtypeStruct((64 * GRAD_ROWS, LANES), F32),
        ),
        in_specs=[WHOLE] * 6,
        out_specs=(WHOLE,) * 2,
        scratch_shapes=[
            pltpu.VMEM((samples, shards * PAD_ROWS), BF),
            pltpu.VMEM((FIELDS, samples, width), F32),
        ],
        compiler_params=PARAMS,
        cost_estimate=cost(6 * samples * shards * PAD_ROWS * h1, 16_000_000),
    )(features, labels.reshape(samples, 1), gathered, w_second, w_third, w_out.reshape(1, h3))
    part = (GRAD_ROWS, LANES)
    row_grad, grad_second, grad_third, grad_out = pl.pallas_call(
        backward_kernel,
        out_shape=(
            jax.ShapeDtypeStruct((touched, width), F32),
            jax.ShapeDtypeStruct((h1, h2), F32),
            jax.ShapeDtypeStruct((h2, h3), F32),
            jax.ShapeDtypeStruct((8, h3), F32),
        ),
        in_specs=[WHOLE] * 4,
        out_specs=(WHOLE,) * 4,
        scratch_shapes=exchange
        + [
            pltpu.SemaphoreType.DMA,
            pltpu.SemaphoreType.DMA((STEPS,)),
            pltpu.VMEM((2, 4, 8) + part, F32),
            pltpu.VMEM((4, 8) + part, F32),
            pltpu.VMEM((4, 8) + part, F32),
            pltpu.VMEM((8,) + part, F32),
            pltpu.VMEM((8,) + part, F32),
            pltpu.VMEM((4, 8) + part, F32),
            pltpu.VMEM((8,) + part, F32),
            pltpu.VMEM(part, F32),
            pltpu.SemaphoreType.DMA((7,)),
            pltpu.SemaphoreType.DMA((7,)),
        ],
        compiler_params=remote_params(1),
        cost_estimate=cost(2 * slots * FIELDS * samples * width, 200_000_000),
    )(numbers, owners, feature_grad, packed.reshape((2, 4, 8) + part))
    return (row_grad, grad_second, grad_third, grad_out[0])


def solution(mesh):
    in_specs = (
        P(("emb", "dp"), None),
        P(("emb", "dp"), None),
        P(("emb", "dp")),
        P(("emb", "dp"), None),
        P(("emb", "dp")),
        P(("emb", "dp")),
        P("emb", None),
        P(),
        P(),
        P(),
    )
    out_specs = (P(("emb", "dp"), None), P(), P(), P())
    return jax.shard_map(
        per_device, mesh=mesh, in_specs=in_specs, out_specs=out_specs, check_vma=False
    )
```

time: 705 us -> 308 us (0.44)
  other arithmetic: 287 us -> 0 us
  Pallas kernels: 0 us -> 237 us
  blocking collectives: 146 us -> 0 us
  local copies, waits for them, and re-layouts: 103 us -> 11 us
  waiting for transfers between devices: 90.6 us -> 45.3 us
  starting transfers between devices: 43.5 us -> 0.04 us
  matrix products: 13.3 us -> 0 us
    pallas_call x0 -> x4, Pallas kernels: none -> 237 us  [the longest x1 126 us: per_device(): pl.pallas_call(backward_kernel, out_shape=(jax.ShapeDtypeStruct((touched,...]
    scatter-add x5 -> x0, other arithmetic: 186 us -> none  [the longest x4 124 us: per_device(): jax.ops.segment_sum(chosen.astype(jnp.float32), piece_ids[:, column], num...]
    psum x1 -> x0, blocking collectives: 146 us -> none  [per_device(): lax.psum((grad_second, grad_third, grad_out), ('emb', 'dp'))]
    scatter x1 -> x0, other arithmetic: 86.9 us -> none  [per_device(): jnp.zeros((shards * capacity, emb_width), jnp.bfloat16).at[slot_index]]
    all_to_all x3 -> x0, waiting for transfers between devices: 59.2 us -> none  [the longest x1 59.2 us: per_device(): lax.all_to_all(outgoing.reshape(shards, capacity, emb_width), 'emb', spli...]
    all_gather x1, waiting for transfers between devices: 0.02 us -> 45.3 us  [per_device(): lax.all_gather(jnp.pad(w_first, ((0, PAD_ROWS - SHARD_ROWS), (0, 0))), 'e...]
    all_to_all x3 -> x0, starting transfers between devices: 43.4 us -> none  [the longest x1 19.1 us: per_device(): lax.all_to_all(slot_owner.reshape(shards, capacity), 'emb', split_axis=0,...]
    gather x2 -> x0, local copies, waits for them, and re-layouts: 31.3 us -> none  [the longest x1 20.8 us: per_device(): returned = padded[flat_owner].reshape(shards, capacity, emb_width)]
  transfers between devices with their start and end apart: 5 -> 1, of which waited for: 2 -> 1; matrix products, arithmetic and copies ran while one was open for 49% -> 1% of each run, Pallas kernels for 0% -> 31%
where the time goes in v1:
time: 308 us; the launch traced here: 307 us
  Pallas kernels  237 us (77%)
  waiting for transfers between devices  45.3 us (15%)
  between operations  14.1 us (5%)
  local copies, waits for them, and re-layouts  11 us (4%)
    pallas_call x1, Pallas kernels, per_device(): pl.pallas_call(backward_kernel, out_shape=(jax.ShapeDtypeStruct((touched,...  126 us
    pallas_call x1, Pallas kernels, per_device(): pl.pallas_call(forward_kernel, out_shape=(jax.ShapeDtypeStruct((samples,...  88.8 us
    all_gather x1, waiting for transfers between devices, per_device(): lax.all_gather(jnp.pad(w_first, ((0, PAD_ROWS - SHARD_ROWS), (0, 0))), 'e...  45.3 us
    pallas_call x1, Pallas kernels, per_device(): pl.pallas_call(dense_kernel, out_shape=(jax.ShapeDtypeStruct((FIELDS * sa...  16 us
  transfers between devices with their start and end apart: 1, of which 1 were waited for; matrix products, arithmetic and copies ran while one was open for 1% of the time, Pallas kernels for 31%

profile of v1, /device:TPU:1, one launch (start us, length us, event | category | flops | bytes accessed | tf_op | source)
XLA Modules:
  0.0 307.2 jit_solution(3035761105717287887)
XLA Ops:
  7.2 0.0 all-gather.2.cloned.1.call-start
  7.2 1.5 pad.4
  8.7 0.0 all-gather.2.cloned.1.call-update
  8.7 0.7 reshape.27.target_ref
  9.5 0.7 reshape.28.count_ref
  10.2 0.8 copy.14.label_ref
  11.0 0.7 reshape.30.last_ref
  11.6 0.0 copy-start.3
  11.6 0.9 copy-done.3
  12.5 0.0 copy-start.4
  12.5 0.7 copy-done.4
  13.2 0.0 copy-start.2
  13.2 6.1 %shard_map.129.numbers_ref = f32[10,128,128]{2,1,0:T(8,128)S(1)} custom-call(s32[1,4992]{1,0:T(1,128)S(1)} %bitcast.6, s32[1,4992]{1,0:T(1,128)S(1)} %reshape.27.target_ref, s32[1,4992]{1,0:T(1,128)S(1)} %reshape.28.count_ref, s32[4,4992]{1,0:T(4,128)S(1)} %bitcast.5), custom_call_target="tpu_custom_call" | custom-call | flops 2126512128 | bytes 2000000 | tf_op jit(solution)/shard_map/pallas_call | solution.py:504
  19.4 0.0 copy-done.2
  19.4 0.0 copy-start
  19.4 0.0 copy-start.1
  19.4 88.8 %shard_map.130 = (bf16[128,3328]{1,0:T(8,128)(2,1)S(1)}, f32[2,128,128]{2,1,0:T(8,128)S(1)}) custom-call(f32[10,128,128]{2,1,0:T(8,128)S(1)} %shard_map.129.numbers_ref, bf16[512,128]{1,0:T(8,128)(2,1)S(1)} %copy-done.2), custom_call_target="tpu_custom_call" | custom-call | flops 8724152320 | bytes 200000000 | tf_op jit(solution)/shard_map/pallas_call | solution.py:521
  108.2 45.3 %all-gather.2.cloned.1.call-done.first_ref = bf16[4096,1024]{1,0:T(8,128)(2,1)} async-done(((bf16[32,1024]{1,0:T(8,128)(2,1)}), bf16[4096,1024]{1,0:T(8,128)(2,1)}) %all-gather.2.cloned.1.call-update) | async-done | bytes 8388624 | tf_op jit(solution)/shard_map/all_gather | solution.py:501
  153.5 0.0 copy-done
  153.5 0.0 copy-done.1
  153.5 16.0 %shard_map.131 = (bf16[3328,128]{1,0:T(8,128)(2,1)S(1)}, f32[5632,128]{1,0:T(8,128)S(1)}) custom-call(bf16[128,3328]{1,0:T(8,128)(2,1)S(1)} %get-tuple-element.13.feature_ref, s32[128,1]{1,0:T(8,128)S(1)} %copy.14.label_ref, bf16[4096,1024]{1,0:T(8,128)(2,1)} %all-gather.2.cloned.1.call-done.first_ref, bf16[1024,512]{1,0:T(8,128)(2,1)S(1)} %copy-done, ...), custom_call_target="tpu_custom_call" | custom-call | flops 3221225472 | bytes 16000000 | tf_op jit(solution)/shard_map/pallas_call | solution.py:538
  169.5 0.0 copy-start.5
  169.5 1.6 copy-done.5
  171.1 125.9 %shard_map.132 = (f32[512,128]{1,0:T(8,128)S(1)}, f32[1024,512]{1,0:T(8,128)S(1)}, f32[512,256]{1,0:T(8,128)S(1)}, f32[8,256]{1,0:T(8,128)S(1)}) custom-call(f32[10,128,128]{2,1,0:T(8,128)S(1)} %shard_map.129.numbers_ref, f32[2,128,128]{2,1,0:T(8,128)S(1)} %get-tuple-element.12.owners_ref, bf16[3328,128]{1,0:T(8,128)(2,1)S(1)} %get-tuple-element.14.grad_ref, ...), custom_call_target="tpu_custom_call" | custom-call | flops 8724152320 | bytes 200000000 | tf_op jit(solution)/shard_map/pallas_call | solution.py:554
  297.0 0.6 slice.3
  297.5 0.7 copy.18
  298.2 1.3 copy.19
  299.6 0.8 copy.20
Async XLA Ops:
  7.2 146.4 %all-gather.2.cloned.1.call-start = ((), (), s32[]{:S(2)}) async-start(), calls=%async_computation | async-start | bytes 8454144 | tf_op jit(solution)/shard_map/all_gather | solution.py:501
  11.6 0.9 copy-start.3
  12.5 0.7 copy-start.4
  13.2 6.2 %copy-start.2 = (bf16[512,128]{1,0:T(8,128)(2,1)S(1)}, bf16[512,128]{1,0:T(8,128)(2,1)}, u32[]{:S(2)}) copy-start(bf16[512,128]{1,0:T(8,128)(2,1)} %rows_ref.1) | copy-start | bytes 393220
  19.4 134.1 %copy-start = (bf16[1024,512]{1,0:T(8,128)(2,1)S(1)}, bf16[1024,512]{1,0:T(8,128)(2,1)}, u32[]{:S(2)}) copy-start(bf16[1024,512]{1,0:T(8,128)(2,1)} %second_ref.1) | copy-start | bytes 3145732
  19.4 134.1 %copy-start.1 = (bf16[512,256]{1,0:T(8,128)(2,1)S(1)}, bf16[512,256]{1,0:T(8,128)(2,1)}, u32[]{:S(2)}) copy-start(bf16[512,256]{1,0:T(8,128)(2,1)} %third_ref.1) | copy-start | bytes 786436
  169.5 1.6 copy-start.5
Sparse Core Ops, SparseCore 0:
  11.7 141.7 all-gather.1

commit v2 on v1

--- a/solution.py
+++ b/solution.py
@@ -93,6 +93,7 @@
 
 
 STEPS = 32
+LAG = 10
 
 
 def quad(step):
@@ -149,14 +150,101 @@
         away()
 
 
+def gather_steps(shard_ref, full_ref, send_sem, recv_sem):
+    emb, x = lax.axis_index("emb"), lax.axis_index("dp")
+    z, y, core = emb // 16, (emb // 2) % 8, emb % 2
+    other = device(core=1 - core)
+    first, second = 2 * x, 2 * x + 1
+
+    def start():
+        for block in (first, second):
+            full_ref[block, z, y, core] = shard_ref[block]
+        for step in range(1, 8):
+            mine = full_ref.at[first, z, y, core]
+            send_to(device(z=(z + step) % 8), mine, mine, send_sem.at[0], recv_sem.at[0])
+            mine = full_ref.at[second, z, y, core]
+            send_to(device(y=(y + step) % 8), mine, mine, send_sem.at[1], recv_sem.at[1])
+
+    def lines():
+        wait_for(full_ref.at[first, pl.ds(0, 7), y, core], recv_sem.at[0])
+        wait_for(full_ref.at[second, z, pl.ds(0, 7), core], recv_sem.at[1])
+        for step in range(1, 8):
+            mine = full_ref.at[first, :, y, core]
+            send_to(device(y=(y + step) % 8), mine, mine, send_sem.at[2], recv_sem.at[2])
+            mine = full_ref.at[second, z, :, core]
+            send_to(device(z=(z + step) % 8), mine, mine, send_sem.at[3], recv_sem.at[3])
+
+    def over_x():
+        wait_for(full_ref.at[first, :, pl.ds(0, 7), core], recv_sem.at[2])
+        wait_for(full_ref.at[second, pl.ds(0, 7), :, core], recv_sem.at[3])
+        mine = full_ref.at[pl.ds(first, 2), :, :, core]
+        for step in range(1, 4):
+            send_to(device(x=(x + step) % 4), mine, mine, send_sem.at[4], recv_sem.at[3 + step])
+        send_to(other, mine, mine, send_sem.at[5], recv_sem.at[7])
+
+    def over_core(step):
+        def forward():
+            mine = full_ref.at[pl.ds(2 * ((x + 4 - step) % 4), 2), :, :, core]
+            wait_for(mine, recv_sem.at[3 + step])
+            send_to(other, mine, mine, send_sem.at[5], recv_sem.at[7])
+
+        return forward
+
+    def finish():
+        wait_for(full_ref.at[:, :, :, core], recv_sem.at[7])
+        wait_for(full_ref.at[first, pl.ds(0, 7), y, core], send_sem.at[0])
+        wait_for(full_ref.at[second, z, pl.ds(0, 7), core], send_sem.at[1])
+        wait_for(full_ref.at[first, :, pl.ds(0, 7), core], send_sem.at[2])
+        wait_for(full_ref.at[second, pl.ds(0, 7), :, core], send_sem.at[3])
+        wait_for(full_ref.at[pl.ds(0, 6), :, :, core], send_sem.at[4])
+        wait_for(full_ref.at[:, :, :, core], send_sem.at[5])
+
+    return [start, lines, over_x, over_core(1), over_core(3), over_core(2), finish]
+
+
+def greet_x(barrier):
+    x = lax.axis_index("dp")
+    for step in range(1, 4):
+        pl.semaphore_signal(
+            barrier,
+            inc=1,
+            device_id=device(x=(x + step) % 4),
+            device_id_type=pl.DeviceIdType.MESH,
+        )
+
+
+def paced_exchange(send, receive, others):
+    def one(step, carry):
+        for at, other in others:
+            pl.when(step == at)(other)
+
+        @pl.when(step < STEPS)
+        def _():
+            send(step)
+
+        @pl.when(step >= LAG)
+        def _():
+            receive(step - LAG)
+
+        return carry
+
+    lax.fori_loop(0, STEPS + LAG, one, 0)
+
+
 def forward_kernel(
-    numbers_ref, rows_ref, out_ref, owners_ref, send_ref, recv_ref, sums_ref, send_sem, recv_sem
+    numbers_ref, rows_ref, shard_ref, out_ref, owners_ref, full_ref,
+    send_ref, recv_ref, sums_ref, send_sem, recv_sem, gather_send, gather_recv,
 ):
     shards = recv_ref.shape[0]
+    gather = gather_steps(shard_ref, full_ref, gather_send, gather_recv)
+    barrier = greet_all()
+    greet_x(barrier)
     recv_ref[:, CAP:] = jnp.zeros((shards, LANES - CAP, LANES), BF)
-    pl.semaphore_wait(greet_all(), LANES - 1)
-
-    def send(step, carry):
+    sums_ref[...] = jnp.zeros_like(sums_ref)
+    pl.semaphore_wait(barrier, LANES - 1 + 3)
+    gather[0]()
+
+    def send(step):
         flip, place, moves = quad(step)
         for which, move in enumerate(moves):
             shard = shard_at(flip, move, 1)
@@ -168,12 +256,8 @@
             tail = jnp.where(end == 7, numbers_ref[1, pl.ds(shard, 1)], tail)
             send_ref[shard] = jnp.concatenate([pooled[: CAP - 8], tail], axis=0).astype(BF)
             send_block(step, which, flip, place, shard, send_ref, recv_ref, send_sem, recv_sem)
-        return carry
-
-    lax.fori_loop(0, STEPS, send, 0)
-    sums_ref[...] = jnp.zeros_like(sums_ref)
-
-    def receive(step, carry):
+
+    def receive(step):
         flip, _, moves = quad(step)
         wait_for(send_ref.at[pl.ds(0, 4)], recv_sem.at[step])
         arrived, fields, samples = [], [], []
@@ -193,12 +277,16 @@
         for tile in range(FIELDS):
             member = in_sample * one_hot(field == tile + 1.0)
             sums_ref[tile] += jnp.dot(member, arrived, preferred_element_type=F32)
-        return carry
-
-    lax.fori_loop(0, STEPS, receive, 0)
+
+    paced_exchange(
+        send,
+        receive,
+        [(1, gather[1]), (8, gather[2]), (32, gather[3]), (34, gather[4]), (38, gather[5])],
+    )
     wait_for(send_ref.at[pl.ds(0, LANES - 1)], send_sem)
     for tile in range(FIELDS):
         out_ref[:, tile * LANES : (tile + 1) * LANES] = sums_ref[tile].astype(BF)
+    gather[6]()
 
 
 def window_tile(tile):
@@ -219,13 +307,20 @@
     feature_ref, label_ref, first_ref, second_ref, third_ref, last_ref,
     grad_ref, packed_ref, padded_ref, network_ref,
 ):
-    padded_tiles = first_ref.shape[0] // LANES
+    blocks, padded_rows, _ = first_ref.shape
+    padded_tiles = padded_rows // LANES
     for tile in range(padded_tiles):
         first, _ = window_tile(tile)
         window = feature_ref[:, first * LANES : (first + 2) * LANES]
         padded = jnp.dot(window, window_map(tile), preferred_element_type=F32)
         padded_ref[:, tile * LANES : (tile + 1) * LANES] = padded.astype(BF)
-    first_pre = jnp.dot(padded_ref[...], first_ref[...], preferred_element_type=F32)
+    first_pre = jnp.concatenate(
+        [
+            jnp.dot(padded_ref[...], first_ref[block], preferred_element_type=F32)
+            for block in range(blocks)
+        ],
+        axis=1,
+    )
     first_act, first_slope = act_slope(first_pre)
     first_act = first_act.astype(BF)
     second_act, second_slope = act_slope(
@@ -253,7 +348,7 @@
     packed_ref[end:] = jnp.zeros_like(packed_ref[end:])
     grad_out = jnp.sum(logit_grad * third_act, axis=0, keepdims=True)
     for tile in range(h3 // LANES):
-        packed_ref[end + 8 * tile : end + 8 * tile + 1] = grad_out[
+        packed_ref[end + 16 * tile : end + 16 * tile + 1] = grad_out[
             :, tile * LANES : (tile + 1) * LANES
         ]
     third_grad = (logit_grad * last * third_slope).astype(BF)
@@ -271,7 +366,9 @@
     network_ref[...] = jnp.zeros_like(network_ref)
     for tile in range(padded_tiles):
         first, _ = window_tile(tile)
-        part = contract(first_grad, first_ref[tile * LANES : (tile + 1) * LANES], 1, 1)
+        rows = slice(tile * LANES, (tile + 1) * LANES)
+        weights = jnp.concatenate([first_ref[block, rows] for block in range(blocks)], axis=1)
+        part = contract(first_grad, weights, 1, 1)
         upper = part.astype(BF)
         lower = (part - upper.astype(F32)).astype(BF)
         place = window_map(tile)
@@ -330,9 +427,8 @@
     def over_z():
         wait_for(from_x.at[pl.ds(0, 3)], recv_sem.at[1])
         for part in range(8):
-            sum_x[part] = (from_x[0, part] + from_x[1, part]) + (
-                from_x[2, part] + from_x[3, part]
-            )
+            total = (from_x[0, part] + from_x[1, part]) + (from_x[2, part] + from_x[3, part])
+            sum_x[part] = total.astype(BF)
         for step in range(1, 8):
             to = (z + step) % 8
             send_to(device(z=to), sum_x.at[to], from_z.at[z], send_sem.at[2], recv_sem.at[2])
@@ -340,7 +436,7 @@
 
     def over_y():
         wait_for(from_z.at[pl.ds(0, 7)], recv_sem.at[2])
-        sum_z[...] = jnp.sum(from_z[...], axis=0)
+        sum_z[...] = jnp.sum(from_z[...].astype(F32), axis=0).astype(BF)
         for step in range(1, 8):
             to = (y + step) % 8
             send_to(device(y=to), sum_z, from_y.at[y], send_sem.at[3], recv_sem.at[3])
@@ -348,7 +444,7 @@
 
     def gather_z():
         wait_for(from_y.at[pl.ds(0, 7)], recv_sem.at[3])
-        full_ref[core, x, z] = jnp.sum(from_y[...], axis=0)
+        full_ref[core, x, z] = jnp.sum(from_y[...].astype(F32), axis=0).astype(BF)
         mine = full_ref.at[core, x, z]
         for step in range(1, 8):
             send_to(device(z=(z + step) % 8), mine, mine, send_sem.at[4], recv_sem.at[4])
@@ -377,44 +473,37 @@
             half, place = divmod(place, 4 * 8 * GRAD_ROWS)
             quarter, place = divmod(place, 8 * GRAD_ROWS)
             part, inside = divmod(place, GRAD_ROWS)
-            ref[row : row + 8, column : column + LANES] = full_ref[
-                half, quarter, part, inside : inside + 8
-            ]
+            block = full_ref[half, quarter, part, inside : inside + 16]
+            ref[row : row + 16, column : column + LANES] = block.astype(F32)
 
     return [over_core, over_x, over_z, over_y, gather_z, gather_x, gather_core, finish]
 
 
-GRAD_ROWS = 88
+GRAD_ROWS = 96
 
 
 def grad_places(second_ref, third_ref, out_ref):
     place = 0
     for ref in (second_ref, third_ref, out_ref):
         for column in range(0, ref.shape[1], LANES):
-            for row in range(0, ref.shape[0], 8):
+            for row in range(0, ref.shape[0], 16):
                 yield place, ref, column, row
-                place += 8
+                place += 16
 
 
 def backward_kernel(
     numbers_ref, owners_ref, grad_ref, packed_ref, out_ref, second_ref, third_ref, last_ref,
     send_ref, recv_ref, send_sem, recv_sem, *reduce_refs,
 ):
-    x, shards = lax.axis_index("dp"), recv_ref.shape[0]
+    shards = recv_ref.shape[0]
+    barrier = greet_all()
+    greet_x(barrier)
     recv_ref[:, CAP:] = jnp.zeros((shards, LANES - CAP, LANES), BF)
     out_ref[...] = jnp.zeros_like(out_ref)
-    barrier = greet_all()
-    for step in range(1, 4):
-        pl.semaphore_signal(
-            barrier,
-            inc=1,
-            device_id=device(x=(x + step) % 4),
-            device_id_type=pl.DeviceIdType.MESH,
-        )
     pl.semaphore_wait(barrier, LANES - 1 + 3)
     reduce = reduce_steps(packed_ref, (second_ref, third_ref, last_ref), *reduce_refs)
 
-    def send(step, carry):
+    def send(step):
         flip, place, moves = quad(step)
         partners = [shard_at(flip, move, 1) for move in moves]
         members = []
@@ -438,9 +527,8 @@
         for which, shard in enumerate(partners):
             send_ref[shard] = spread[which * CAP : (which + 1) * CAP]
             send_block(step, which, flip, place, shard, send_ref, recv_ref, send_sem, recv_sem)
-        return carry
-
-    def receive(step, carry):
+
+    def receive(step):
         flip, _, moves = quad(step)
         wait_for(send_ref.at[pl.ds(0, 4)], recv_sem.at[step])
         partners = [shard_at(flip, move, -1) for move in moves]
@@ -448,17 +536,21 @@
         high, low = number_rows(numbers_ref, partners)
         counts = count_rows(high, low, out_ref.shape[0] // LANES)
         out_ref[...] += jnp.dot(counts, arrived, preferred_element_type=F32)
-        return carry
 
     reduce[0]()
-    lax.fori_loop(0, 8, send, 0)
-    reduce[1]()
-    lax.fori_loop(8, STEPS, send, 0)
-    for part, reduce_step in enumerate(reduce[2:6]):
-        reduce_step()
-        lax.fori_loop(part * 8, part * 8 + 8, receive, 0)
-    for reduce_step in reduce[6:]:
-        reduce_step()
+    paced_exchange(
+        send,
+        receive,
+        [
+            (2, reduce[1]),
+            (10, reduce[2]),
+            (16, reduce[3]),
+            (21, reduce[4]),
+            (26, reduce[5]),
+            (34, reduce[6]),
+        ],
+    )
+    reduce[7]()
     wait_for(send_ref.at[pl.ds(0, LANES - 1)], send_sem)
 
 
@@ -498,9 +590,9 @@
     h3 = w_third.shape[1]
     slots = shards * CAP
 
-    gathered = lax.all_gather(
-        jnp.pad(w_first, ((0, PAD_ROWS - SHARD_ROWS), (0, 0))), "emb", axis=0, tiled=True
-    )
+    blocks = h1 // LANES
+    shard = jnp.pad(w_first, ((0, PAD_ROWS - SHARD_ROWS), (0, 0)))
+    shard = shard.reshape(PAD_ROWS, blocks, LANES).transpose(1, 0, 2)
     numbers = pl.pallas_call(
         slots_kernel,
         out_shape=jax.ShapeDtypeStruct((10, shards, LANES), F32),
@@ -518,23 +610,27 @@
         pltpu.VMEM((shards, CAP, width), BF),
         pltpu.VMEM((shards, LANES, width), BF),
     ]
-    features, owners = pl.pallas_call(
+    features, owners, full = pl.pallas_call(
         forward_kernel,
         out_shape=(
             jax.ShapeDtypeStruct((samples, FIELDS * width), BF),
             jax.ShapeDtypeStruct((2, shards, LANES), F32),
+            jax.ShapeDtypeStruct((blocks, 8, 8, 2, PAD_ROWS, LANES), BF),
         ),
-        in_specs=[WHOLE] * 2,
-        out_specs=(WHOLE,) * 2,
+        in_specs=[WHOLE] * 3,
+        out_specs=(WHOLE,) * 3,
         scratch_shapes=exchange
         + [
             pltpu.VMEM((FIELDS, samples, width), F32),
             pltpu.SemaphoreType.DMA,
             pltpu.SemaphoreType.DMA((STEPS,)),
+            pltpu.SemaphoreType.DMA((6,)),
+            pltpu.SemaphoreType.DMA((8,)),
         ],
         compiler_params=remote_params(0),
         cost_estimate=cost(2 * slots * FIELDS * samples * width, 200_000_000),
-    )(numbers, table_rows)
+    )(numbers, table_rows, shard)
+    full = full.reshape(blocks, shards * PAD_ROWS, LANES)
     feature_grad, packed = pl.pallas_call(
         dense_kernel,
         out_shape=(
@@ -549,7 +645,7 @@
         ],
         compiler_params=PARAMS,
         cost_estimate=cost(6 * samples * shards * PAD_ROWS * h1, 16_000_000),
-    )(features, labels.reshape(samples, 1), gathered, w_second, w_third, w_out.reshape(1, h3))
+    )(features, labels.reshape(samples, 1), full, w_second, w_third, w_out.reshape(1, h3))
     part = (GRAD_ROWS, LANES)
     row_grad, grad_second, grad_third, grad_out = pl.pallas_call(
         backward_kernel,
@@ -557,7 +653,7 @@
             jax.ShapeDtypeStruct((touched, width), F32),
             jax.ShapeDtypeStruct((h1, h2), F32),
             jax.ShapeDtypeStruct((h2, h3), F32),
-            jax.ShapeDtypeStruct((8, h3), F32),
+            jax.ShapeDtypeStruct((16, h3), F32),
         ),
         in_specs=[WHOLE] * 4,
         out_specs=(WHOLE,) * 4,
@@ -565,14 +661,14 @@
         + [
             pltpu.SemaphoreType.DMA,
             pltpu.SemaphoreType.DMA((STEPS,)),
-            pltpu.VMEM((2, 4, 8) + part, F32),
+            pltpu.VMEM((2, 4, 8) + part, BF),
             pltpu.VMEM((4, 8) + part, F32),
             pltpu.VMEM((4, 8) + part, F32),
-            pltpu.VMEM((8,) + part, F32),
-            pltpu.VMEM((8,) + part, F32),
+            pltpu.VMEM((8,) + part, BF),
+            pltpu.VMEM((8,) + part, BF),
             pltpu.VMEM((4, 8) + part, F32),
-            pltpu.VMEM((8,) + part, F32),
-            pltpu.VMEM(part, F32),
+            pltpu.VMEM((8,) + part, BF),
+            pltpu.VMEM(part, BF),
             pltpu.SemaphoreType.DMA((7,)),
             pltpu.SemaphoreType.DMA((7,)),
         ],

time: 308 us -> 242 us (0.79); the launches traced: 307 us -> 238 us
  waiting for transfers between devices: 45.3 us -> 0 us
  between operations: 14.1 us -> 0.72 us
  Pallas kernels: 237 us -> 229 us
    all_gather x1 -> x0, waiting for transfers between devices: 45.3 us -> none  [per_device(): lax.all_gather(jnp.pad(w_first, ((0, PAD_ROWS - SHARD_ROWS), (0, 0))), 'e...]
    pallas_call x1, Pallas kernels: 126 us -> 98.1 us  [per_device(): pl.pallas_call(backward_kernel, out_shape=(jax.ShapeDtypeStruct((touched,...]
    pallas_call x1, Pallas kernels: 88.8 us -> 107 us  [per_device(): pl.pallas_call(forward_kernel, out_shape=(jax.ShapeDtypeStruct((samples,...]
  transfers between devices with their start and end apart: 1 -> 0, of which waited for: 1 -> 0; matrix products, arithmetic and copies ran while one was open for 1% -> 0% of each run, Pallas kernels for 31% -> 0%
where the time goes in v2:
time: 242 us; the launch traced here: 238 us
  Pallas kernels  229 us (95%)
  local copies, waits for them, and re-layouts  8.76 us (4%)
    pallas_call x1, Pallas kernels, per_device(): pl.pallas_call(forward_kernel, out_shape=(jax.ShapeDtypeStruct((samples,...  107 us
    pallas_call x1, Pallas kernels, per_device(): pl.pallas_call(backward_kernel, out_shape=(jax.ShapeDtypeStruct((touched,...  98.1 us
    pallas_call x1, Pallas kernels, per_device(): pl.pallas_call(dense_kernel, out_shape=(jax.ShapeDtypeStruct((FIELDS * sa...  17.1 us
    pallas_call x1, Pallas kernels, per_device(): pl.pallas_call(slots_kernel, out_shape=jax.ShapeDtypeStruct((10, shards,...  6.15 us

profile of v2, /device:TPU:1, one launch (start us, length us, event | category | flops | bytes accessed | tf_op | source)
XLA Modules:
  0.0 238.0 jit_solution(16581667380802923480)
XLA Ops:
  0.6 0.7 reshape.38.last_ref
  1.3 0.7 reshape.34.count_ref
  2.0 0.7 reshape.33.target_ref
  2.8 0.8 copy.16.label_ref
  3.5 0.9 bitcast_bitcast_fusion.shard_ref
  4.4 0.0 copy-start.3
  4.4 0.9 copy-done.3
  5.3 0.0 copy-start.4
  5.3 0.7 copy-done.4
  6.0 0.0 copy-start.2
  6.0 6.1 %shard_map.129.numbers_ref = f32[10,128,128]{2,1,0:T(8,128)S(1)} custom-call(s32[1,4992]{1,0:T(1,128)S(1)} %bitcast.14, s32[1,4992]{1,0:T(1,128)S(1)} %reshape.33.target_ref, s32[1,4992]{1,0:T(1,128)S(1)} %reshape.34.count_ref, s32[4,4992]{1,0:T(4,128)S(1)} %bitcast.13), custom_call_target="tpu_custom_call" | custom-call | flops 2126512128 | bytes 2000000 | tf_op jit(solution)/shard_map/pallas_call | solution.py:596
  12.2 0.0 copy-done.2
  12.2 0.0 copy-start
  12.2 0.0 copy-start.1
  12.2 107.3 %shard_map.130 = (bf16[128,3328]{1,0:T(8,128)(2,1)S(1)}, f32[2,128,128]{2,1,0:T(8,128)S(1)}, bf16[8,8,8,2,32,128]{5,4,3,2,1,0:T(8,128)(2,1)}) custom-call(f32[10,128,128]{2,1,0:T(8,128)S(1)} %shard_map.129.numbers_ref, bf16[512,128]{1,0:T(8,128)(2,1)S(1)} %copy-done.2, bf16[8,32,128]{2,1,0:T(8,128)(2,1)S(1)} %bitcast_bitcast_fusion.shard_ref), custom_call_target="tpu_custom_call" | custom-call | flops 8724152320 | bytes 200000000 | tf_op jit(solution)/shard_map/pallas_call | solution.py:613
  119.5 0.0 copy-done
  119.5 0.0 copy-done.1
  119.5 17.1 %shard_map.131 = (bf16[3328,128]{1,0:T(8,128)(2,1)S(1)}, f32[6144,128]{1,0:T(8,128)}) custom-call(bf16[128,3328]{1,0:T(8,128)(2,1)S(1)} %get-tuple-element.14.feature_ref, s32[128,1]{1,0:T(8,128)S(1)} %copy.16.label_ref, bf16[8,4096,128]{2,1,0:T(8,128)(2,1)} %bitcast.17, bf16[1024,512]{1,0:T(8,128)(2,1)S(1)} %copy-done, bf16[512,256]{1,0:T(8,128)(2,1)S(1)} %copy-done.1, ...), custom_call_target="tpu_custom_call" | custom-call | flops 3221225472 | bytes 16000000 | tf_op jit(solution)/shard_map/pallas_call | solution.py:634
  136.6 98.1 %shard_map.132 = (f32[512,128]{1,0:T(8,128)S(1)}, f32[1024,512]{1,0:T(8,128)S(1)}, f32[512,256]{1,0:T(8,128)S(1)}, f32[16,256]{1,0:T(8,128)S(1)}) custom-call(f32[10,128,128]{2,1,0:T(8,128)S(1)} %shard_map.129.numbers_ref, f32[2,128,128]{2,1,0:T(8,128)S(1)} %get-tuple-element.13.owners_ref, bf16[3328,128]{1,0:T(8,128)(2,1)S(1)} %get-tuple-element.16.grad_ref, ...), custom_call_target="tpu_custom_call" | custom-call | flops 8724152320 | bytes 200000000 | tf_op jit(solution)/shard_map/pallas_call | solution.py:650
  234.6 0.6 slice.3
  235.2 0.7 copy.22
  235.9 1.3 copy.23
  237.2 0.8 copy.24
Async XLA Ops:
  4.4 0.9 copy-start.3
  5.3 0.7 copy-start.4
  6.0 6.2 %copy-start.2 = (bf16[512,128]{1,0:T(8,128)(2,1)S(1)}, bf16[512,128]{1,0:T(8,128)(2,1)}, u32[]{:S(2)}) copy-start(bf16[512,128]{1,0:T(8,128)(2,1)} %rows_ref.1) | copy-start | bytes 393220
  12.2 107.3 %copy-start = (bf16[1024,512]{1,0:T(8,128)(2,1)S(1)}, bf16[1024,512]{1,0:T(8,128)(2,1)}, u32[]{:S(2)}) copy-start(bf16[1024,512]{1,0:T(8,128)(2,1)} %second_ref.1) | copy-start | bytes 3145732
  12.2 107.3 %copy-start.1 = (bf16[512,256]{1,0:T(8,128)(2,1)S(1)}, bf16[512,256]{1,0:T(8,128)(2,1)}, u32[]{:S(2)}) copy-start(bf16[512,256]{1,0:T(8,128)(2,1)} %third_ref.1) | copy-start | bytes 786436

commit v3 on v2

--- a/solution.py
+++ b/solution.py
@@ -42,7 +42,7 @@
     return jnp.where(condition, 1.0, 0.0).astype(BF)
 
 
-def slots_kernel(dest_ref, target_ref, count_ref, ids_ref, slots_ref):
+def fill_slots(dest_ref, target_ref, count_ref, ids_ref, slots_ref):
     pieces = dest_ref.shape[1]
     shards = slots_ref.shape[1]
     chunk = PIECE_CHUNK
@@ -58,14 +58,14 @@
         carry = carry + jnp.sum(is_dest, axis=1, keepdims=True)
         at_rank = one_hot(iota((LANES, chunk), 0).astype(F32) == rank)
         target = target_ref[:, part]
-        sample = (target * 2521) // 65536
+        sample = (target * 2521) >> 16
         field = target - sample * FIELDS
         count = count_ref[:, part]
         numbers = [field + 1, sample]
         for column in range(ids_ref.shape[0]):
             ids = ids_ref[column : column + 1, part]
-            numbers.append(jnp.where(column < count, ids // LANES + 1, 0))
-            numbers.append(ids % LANES)
+            numbers.append(jnp.where(column < count, (ids >> 7) + 1, 0))
+            numbers.append(ids & (LANES - 1))
         scaled = jnp.concatenate(
             [to_dest * number.astype(F32).astype(BF) for number in numbers], axis=0
         )
@@ -231,19 +231,45 @@
     lax.fori_loop(0, STEPS + LAG, one, 0)
 
 
-def forward_kernel(
-    numbers_ref, rows_ref, shard_ref, out_ref, owners_ref, full_ref,
-    send_ref, recv_ref, sums_ref, send_sem, recv_sem, gather_send, gather_recv,
+def step_kernel(
+    dest_ref, target_ref, count_ref, ids_ref, rows_ref, shard_ref, label_ref, second_ref,
+    third_ref, last_ref,
+    row_grad_ref, grad_second_ref, grad_third_ref, grad_out_ref,
+    numbers_ref, owners_ref, full_ref, feature_ref, grad_ref, packed_ref, padded_ref, sums_ref,
+    send_ref, recv_ref, back_ref, send_sem, recv_sem, back_send_sem, back_recv_sem,
+    gather_send, gather_recv, *reduce_refs,
 ):
-    shards = recv_ref.shape[0]
     gather = gather_steps(shard_ref, full_ref, gather_send, gather_recv)
+    outs = (grad_second_ref, grad_third_ref, grad_out_ref)
+    reduce = reduce_steps(packed_ref, outs, *reduce_refs)
     barrier = greet_all()
     greet_x(barrier)
-    recv_ref[:, CAP:] = jnp.zeros((shards, LANES - CAP, LANES), BF)
+    empty = jnp.zeros((recv_ref.shape[0], LANES - CAP, LANES), BF)
+    recv_ref[:, CAP:] = empty
+    back_ref[:, CAP:] = empty
     sums_ref[...] = jnp.zeros_like(sums_ref)
+    row_grad_ref[...] = jnp.zeros_like(row_grad_ref)
+    fill_slots(dest_ref, target_ref, count_ref, ids_ref, numbers_ref)
     pl.semaphore_wait(barrier, LANES - 1 + 3)
     gather[0]()
-
+    forward_exchange(
+        numbers_ref, rows_ref, feature_ref, owners_ref, send_ref, recv_ref, sums_ref,
+        send_sem, recv_sem, gather,
+    )
+    dense_step(
+        feature_ref, label_ref, full_ref, second_ref, third_ref, last_ref,
+        grad_ref, packed_ref, padded_ref, sums_ref, reduce[0],
+    )
+    backward_exchange(
+        numbers_ref, owners_ref, grad_ref, row_grad_ref, send_ref, back_ref,
+        back_send_sem, back_recv_sem, reduce,
+    )
+
+
+def forward_exchange(
+    numbers_ref, rows_ref, out_ref, owners_ref, send_ref, recv_ref, sums_ref,
+    send_sem, recv_sem, gather,
+):
     def send(step):
         flip, place, moves = quad(step)
         for which, move in enumerate(moves):
@@ -303,11 +329,11 @@
     return jnp.where(row < SHARD_ROWS, one_hot(feature == wanted), jnp.zeros((), BF))
 
 
-def dense_kernel(
+def dense_step(
     feature_ref, label_ref, first_ref, second_ref, third_ref, last_ref,
-    grad_ref, packed_ref, padded_ref, network_ref,
+    grad_ref, packed_ref, padded_ref, network_ref, after_sums,
 ):
-    blocks, padded_rows, _ = first_ref.shape
+    blocks, padded_rows = first_ref.shape[0], padded_ref.shape[1]
     padded_tiles = padded_rows // LANES
     for tile in range(padded_tiles):
         first, _ = window_tile(tile)
@@ -316,7 +342,11 @@
         padded_ref[:, tile * LANES : (tile + 1) * LANES] = padded.astype(BF)
     first_pre = jnp.concatenate(
         [
-            jnp.dot(padded_ref[...], first_ref[block], preferred_element_type=F32)
+            jnp.dot(
+                padded_ref[...],
+                first_ref[block].reshape(padded_rows, LANES),
+                preferred_element_type=F32,
+            )
             for block in range(blocks)
         ],
         axis=1,
@@ -362,12 +392,14 @@
         packed_ref[tile * h1 : (tile + 1) * h1] = contract(
             first_act, second_grad[:, tile * LANES : (tile + 1) * LANES], 0, 0
         )
+    after_sums()
     first_grad = (contract(second_grad, second_ref[...], 1, 1) * first_slope).astype(BF)
     network_ref[...] = jnp.zeros_like(network_ref)
     for tile in range(padded_tiles):
         first, _ = window_tile(tile)
-        rows = slice(tile * LANES, (tile + 1) * LANES)
-        weights = jnp.concatenate([first_ref[block, rows] for block in range(blocks)], axis=1)
+        z, y = tile // 4, tile % 4 * 2
+        weights = [first_ref[block, z, y : y + 2] for block in range(blocks)]
+        weights = jnp.concatenate([one.reshape(LANES, LANES) for one in weights], axis=1)
         part = contract(first_grad, weights, 1, 1)
         upper = part.astype(BF)
         lower = (part - upper.astype(F32)).astype(BF)
@@ -411,14 +443,19 @@
     emb, x = lax.axis_index("emb"), lax.axis_index("dp")
     z, y, core = emb // 16, (emb // 2) % 8, emb % 2
     other = device(core=1 - core)
+    half = packed_ref.shape[0] // 2
+    eighth = half // 4
 
     def over_core():
-        send_to(other, packed_ref.at[1 - core], from_core, send_sem.at[0], recv_sem.at[0])
+        theirs = packed_ref.at[pl.ds(pl.multiple_of((1 - core) * half, eighth), half)]
+        send_to(other, theirs, from_core, send_sem.at[0], recv_sem.at[0])
 
     def over_x():
         wait_for(from_core, recv_sem.at[0])
         for part in range(4):
-            sum_core[part] = packed_ref[core, part] + from_core[part]
+            mine = packed_ref[pl.ds(pl.multiple_of(core * half + part * eighth, eighth), eighth)]
+            theirs = from_core[part * eighth : (part + 1) * eighth]
+            sum_core[part] = (mine + theirs).reshape(sum_core.shape[1:])
         for step in range(1, 4):
             to = (x + step) % 4
             send_to(device(x=to), sum_core.at[to], from_x.at[x], send_sem.at[1], recv_sem.at[1])
@@ -491,18 +528,9 @@
                 place += 16
 
 
-def backward_kernel(
-    numbers_ref, owners_ref, grad_ref, packed_ref, out_ref, second_ref, third_ref, last_ref,
-    send_ref, recv_ref, send_sem, recv_sem, *reduce_refs,
+def backward_exchange(
+    numbers_ref, owners_ref, grad_ref, out_ref, send_ref, recv_ref, send_sem, recv_sem, reduce
 ):
-    shards = recv_ref.shape[0]
-    barrier = greet_all()
-    greet_x(barrier)
-    recv_ref[:, CAP:] = jnp.zeros((shards, LANES - CAP, LANES), BF)
-    out_ref[...] = jnp.zeros_like(out_ref)
-    pl.semaphore_wait(barrier, LANES - 1 + 3)
-    reduce = reduce_steps(packed_ref, (second_ref, third_ref, last_ref), *reduce_refs)
-
     def send(step):
         flip, place, moves = quad(step)
         partners = [shard_at(flip, move, 1) for move in moves]
@@ -537,7 +565,6 @@
         counts = count_rows(high, low, out_ref.shape[0] // LANES)
         out_ref[...] += jnp.dot(counts, arrived, preferred_element_type=F32)
 
-    reduce[0]()
     paced_exchange(
         send,
         receive,
@@ -554,12 +581,9 @@
     wait_for(send_ref.at[pl.ds(0, LANES - 1)], send_sem)
 
 
-PARAMS = pltpu.CompilerParams(vmem_limit_bytes=48 << 20)
-
-
 def remote_params(collective_id):
     return pltpu.CompilerParams(
-        vmem_limit_bytes=48 << 20, collective_id=collective_id, has_side_effects=True
+        vmem_limit_bytes=56 << 20, collective_id=collective_id, has_side_effects=True
     )
 
 
@@ -588,81 +612,42 @@
     samples = labels.shape[0]
     h1, h2 = w_second.shape
     h3 = w_third.shape[1]
-    slots = shards * CAP
 
     blocks = h1 // LANES
+    padded = shards * PAD_ROWS
     shard = jnp.pad(w_first, ((0, PAD_ROWS - SHARD_ROWS), (0, 0)))
     shard = shard.reshape(PAD_ROWS, blocks, LANES).transpose(1, 0, 2)
-    numbers = pl.pallas_call(
-        slots_kernel,
-        out_shape=jax.ShapeDtypeStruct((10, shards, LANES), F32),
-        in_specs=[WHOLE] * 4,
-        out_specs=WHOLE,
-        compiler_params=PARAMS,
-        cost_estimate=cost(2 * 1664 * pieces * LANES, 2_000_000),
-    )(
-        piece_dest.reshape(1, pieces),
-        piece_target.reshape(1, pieces),
-        piece_counts.reshape(1, pieces),
-        piece_ids.T,
-    )
-    exchange = [
-        pltpu.VMEM((shards, CAP, width), BF),
-        pltpu.VMEM((shards, LANES, width), BF),
-    ]
-    features, owners, full = pl.pallas_call(
-        forward_kernel,
-        out_shape=(
-            jax.ShapeDtypeStruct((samples, FIELDS * width), BF),
-            jax.ShapeDtypeStruct((2, shards, LANES), F32),
-            jax.ShapeDtypeStruct((blocks, 8, 8, 2, PAD_ROWS, LANES), BF),
-        ),
-        in_specs=[WHOLE] * 3,
-        out_specs=(WHOLE,) * 3,
-        scratch_shapes=exchange
-        + [
-            pltpu.VMEM((FIELDS, samples, width), F32),
-            pltpu.SemaphoreType.DMA,
-            pltpu.SemaphoreType.DMA((STEPS,)),
-            pltpu.SemaphoreType.DMA((6,)),
-            pltpu.SemaphoreType.DMA((8,)),
-        ],
-        compiler_params=remote_params(0),
-        cost_estimate=cost(2 * slots * FIELDS * samples * width, 200_000_000),
-    )(numbers, table_rows, shard)
-    full = full.reshape(blocks, shards * PAD_ROWS, LANES)
-    feature_grad, packed = pl.pallas_call(
-        dense_kernel,
-        out_shape=(
-            jax.ShapeDtypeStruct((FIELDS * samples, width), BF),
-            jax.ShapeDtypeStruct((64 * GRAD_ROWS, LANES), F32),
-        ),
-        in_specs=[WHOLE] * 6,
-        out_specs=(WHOLE,) * 2,
-        scratch_shapes=[
-            pltpu.VMEM((samples, shards * PAD_ROWS), BF),
-            pltpu.VMEM((FIELDS, samples, width), F32),
-        ],
-        compiler_params=PARAMS,
-        cost_estimate=cost(6 * samples * shards * PAD_ROWS * h1, 16_000_000),
-    )(features, labels.reshape(samples, 1), full, w_second, w_third, w_out.reshape(1, h3))
     part = (GRAD_ROWS, LANES)
     row_grad, grad_second, grad_third, grad_out = pl.pallas_call(
-        backward_kernel,
+        step_kernel,
         out_shape=(
             jax.ShapeDtypeStruct((touched, width), F32),
             jax.ShapeDtypeStruct((h1, h2), F32),
             jax.ShapeDtypeStruct((h2, h3), F32),
             jax.ShapeDtypeStruct((16, h3), F32),
         ),
-        in_specs=[WHOLE] * 4,
+        in_specs=[WHOLE] * 10,
         out_specs=(WHOLE,) * 4,
-        scratch_shapes=exchange
-        + [
+        scratch_shapes=[
+            pltpu.VMEM((10, shards, LANES), F32),
+            pltpu.VMEM((2, shards, LANES), F32),
+            pltpu.VMEM((blocks, 8, 8, 2, PAD_ROWS, LANES), BF),
+            pltpu.VMEM((samples, FIELDS * width), BF),
+            pltpu.VMEM((FIELDS * samples, width), BF),
+            pltpu.VMEM((64 * GRAD_ROWS, LANES), F32),
+            pltpu.VMEM((samples, padded), BF),
+            pltpu.VMEM((FIELDS, samples, width), F32),
+            pltpu.VMEM((shards, CAP, width), BF),
+            pltpu.VMEM((shards, LANES, width), BF),
+            pltpu.VMEM((shards, LANES, width), BF),
             pltpu.SemaphoreType.DMA,
             pltpu.SemaphoreType.DMA((STEPS,)),
+            pltpu.SemaphoreType.DMA,
+            pltpu.SemaphoreType.DMA((STEPS,)),
+            pltpu.SemaphoreType.DMA((6,)),
+            pltpu.SemaphoreType.DMA((8,)),
             pltpu.VMEM((2, 4, 8) + part, BF),
-            pltpu.VMEM((4, 8) + part, F32),
+            pltpu.VMEM((32 * GRAD_ROWS, LANES), F32),
             pltpu.VMEM((4, 8) + part, F32),
             pltpu.VMEM((8,) + part, BF),
             pltpu.VMEM((8,) + part, BF),
@@ -672,9 +657,20 @@
             pltpu.SemaphoreType.DMA((7,)),
             pltpu.SemaphoreType.DMA((7,)),
         ],
-        compiler_params=remote_params(1),
-        cost_estimate=cost(2 * slots * FIELDS * samples * width, 200_000_000),
-    )(numbers, owners, feature_grad, packed.reshape((2, 4, 8) + part))
+        compiler_params=remote_params(0),
+        cost_estimate=cost(4 * shards * CAP * FIELDS * samples * width, 400_000_000),
+    )(
+        piece_dest.reshape(1, pieces),
+        piece_target.reshape(1, pieces),
+        piece_counts.reshape(1, pieces),
+        piece_ids.T,
+        table_rows,
+        shard,
+        labels.reshape(samples, 1),
+        w_second,
+        w_third,
+        w_out.reshape(1, h3),
+    )
     return (row_grad, grad_second, grad_third, grad_out[0])
 
 

time: 242 us -> 220 us (0.909); the launches traced: 238 us -> 219 us
  Pallas kernels: 229 us -> 205 us
  local copies, waits for them, and re-layouts: 8.76 us -> 13.6 us
    pallas_call x4 -> x1, Pallas kernels: 229 us -> 205 us  [per_device(): pl.pallas_call(step_kernel, out_shape=(jax.ShapeDtypeStruct((touched, wid...]
    unnamed x13 -> x5, local copies, waits for them, and re-layouts: 4.44 us -> 5.6 us
where the time goes in v3:
time: 220 us; the launch traced here: 219 us
  Pallas kernels  205 us (93%)
  local copies, waits for them, and re-layouts  13.6 us (6%)
    pallas_call x1, Pallas kernels, per_device(): pl.pallas_call(step_kernel, out_shape=(jax.ShapeDtypeStruct((touched, wid...  205 us
    unnamed x5, local copies, waits for them, and re-layouts  5.6 us

profile of v3, /device:TPU:1, one launch (start us, length us, event | category | flops | bytes accessed | tf_op | source)
XLA Modules:
  0.0 219.0 jit_solution(8273329912315677002)
XLA Ops:
  0.6 1.2 reshape.31.last_ref
  1.9 1.3 reshape.28.count_ref
  3.2 1.3 reshape.27.target_ref
  4.5 1.4 copy.16.label_ref
  5.9 1.5 bitcast_bitcast_fusion.shard_ref
  7.4 204.7 %shard_map.129 = (f32[512,128]{1,0:T(8,128)}, f32[1024,512]{1,0:T(8,128)}, f32[512,256]{1,0:T(8,128)}, f32[16,256]{1,0:T(8,128)}) custom-call(s32[1,4992]{1,0:T(1,128)} %bitcast.14, s32[1,4992]{1,0:T(1,128)} %reshape.27.target_ref, s32[1,4992]{1,0:T(1,128)} %reshape.28.count_ref, s32[4,4992]{1,0:T(4,128)} %bitcast.13, bf16[512,128]{1,0:T(8,128)(2,1)} %rows_ref.1, ...), custom_call_target="tpu_custom_call" | custom-call | flops 17448304640 | bytes 400000000 | tf_op jit(solution)/shard_map/pallas_call | solution.py:621
  212.1 1.3 slice.3
  213.3 1.7 copy.22
  215.0 0.0 copy-start
  215.0 3.1 %copy.23 = f32[1024,512]{1,0:T(8,128)} copy(f32[1024,512]{1,0:T(8,128)} %get-tuple-element.17) | data formatting | bytes 4194304
  218.2 0.0 copy-done
  218.2 0.8 copy.24
Async XLA Ops:
  215.0 3.1 %copy-start = (f32[512,256]{1,0:T(8,128)S(1)}, f32[512,256]{1,0:T(8,128)}, u32[]{:S(2)}) copy-start(f32[512,256]{1,0:T(8,128)} %get-tuple-element.18) | copy-start | bytes 1572868

commit v4 on v3

--- a/solution.py
+++ b/solution.py
@@ -40,6 +40,11 @@
 
 def one_hot(condition):
     return jnp.where(condition, 1.0, 0.0).astype(BF)
+
+
+def flat_part(ref, step):
+    rows = range(step * PIECE_CHUNK // LANES, (step + 1) * PIECE_CHUNK // LANES)
+    return jnp.concatenate([ref[row : row + 1] for row in rows], axis=1)
 
 
 def fill_slots(dest_ref, target_ref, count_ref, ids_ref, slots_ref):
@@ -57,10 +62,10 @@
         rank = jnp.sum(is_dest * earlier, axis=0, keepdims=True)
         carry = carry + jnp.sum(is_dest, axis=1, keepdims=True)
         at_rank = one_hot(iota((LANES, chunk), 0).astype(F32) == rank)
-        target = target_ref[:, part]
+        target = flat_part(target_ref, step)
         sample = (target * 2521) >> 16
         field = target - sample * FIELDS
-        count = count_ref[:, part]
+        count = flat_part(count_ref, step)
         numbers = [field + 1, sample]
         for column in range(ids_ref.shape[0]):
             ids = ids_ref[column : column + 1, part]
@@ -93,7 +98,7 @@
 
 
 STEPS = 32
-LAG = 10
+LAG = 12
 
 
 def quad(step):
@@ -155,43 +160,54 @@
     z, y, core = emb // 16, (emb // 2) % 8, emb % 2
     other = device(core=1 - core)
     first, second = 2 * x, 2 * x + 1
+    right, left = (x + 1) % 4, (x + 3) % 4
+
+    def mine(whose):
+        return full_ref.at[pl.ds(2 * whose, 2), :, :, core]
 
     def start():
         for block in (first, second):
             full_ref[block, z, y, core] = shard_ref[block]
         for step in range(1, 8):
-            mine = full_ref.at[first, z, y, core]
-            send_to(device(z=(z + step) % 8), mine, mine, send_sem.at[0], recv_sem.at[0])
-            mine = full_ref.at[second, z, y, core]
-            send_to(device(y=(y + step) % 8), mine, mine, send_sem.at[1], recv_sem.at[1])
+            block_here = full_ref.at[first, z, y, core]
+            send_to(device(z=(z + step) % 8), block_here, block_here, send_sem.at[0], recv_sem.at[0])
+            block_here = full_ref.at[second, z, y, core]
+            send_to(device(y=(y + step) % 8), block_here, block_here, send_sem.at[1], recv_sem.at[1])
 
     def lines():
         wait_for(full_ref.at[first, pl.ds(0, 7), y, core], recv_sem.at[0])
         wait_for(full_ref.at[second, z, pl.ds(0, 7), core], recv_sem.at[1])
         for step in range(1, 8):
-            mine = full_ref.at[first, :, y, core]
-            send_to(device(y=(y + step) % 8), mine, mine, send_sem.at[2], recv_sem.at[2])
-            mine = full_ref.at[second, z, :, core]
-            send_to(device(z=(z + step) % 8), mine, mine, send_sem.at[3], recv_sem.at[3])
+            block_here = full_ref.at[first, :, y, core]
+            send_to(device(y=(y + step) % 8), block_here, block_here, send_sem.at[2], recv_sem.at[2])
+            block_here = full_ref.at[second, z, :, core]
+            send_to(device(z=(z + step) % 8), block_here, block_here, send_sem.at[3], recv_sem.at[3])
 
     def over_x():
         wait_for(full_ref.at[first, :, pl.ds(0, 7), core], recv_sem.at[2])
         wait_for(full_ref.at[second, pl.ds(0, 7), :, core], recv_sem.at[3])
-        mine = full_ref.at[pl.ds(first, 2), :, :, core]
-        for step in range(1, 4):
-            send_to(device(x=(x + step) % 4), mine, mine, send_sem.at[4], recv_sem.at[3 + step])
-        send_to(other, mine, mine, send_sem.at[5], recv_sem.at[7])
-
-    def over_core(step):
-        def forward():
-            mine = full_ref.at[pl.ds(2 * ((x + 4 - step) % 4), 2), :, :, core]
-            wait_for(mine, recv_sem.at[3 + step])
-            send_to(other, mine, mine, send_sem.at[5], recv_sem.at[7])
-
-        return forward
+        send_to(device(x=right), mine(x), mine(x), send_sem.at[4], recv_sem.at[4])
+        send_to(device(x=left), mine(x), mine(x), send_sem.at[4], recv_sem.at[5])
+        send_to(other, mine(x), mine(x), send_sem.at[5], recv_sem.at[8])
+
+    def forward():
+        wait_for(mine(left), recv_sem.at[4])
+        block = full_ref.at[2 * left, :, :, core]
+        send_to(device(x=right), block, block, send_sem.at[4], recv_sem.at[6])
+        wait_for(mine(right), recv_sem.at[5])
+        block = full_ref.at[2 * right + 1, :, :, core]
+        send_to(device(x=left), block, block, send_sem.at[4], recv_sem.at[7])
+        for near in (left, right):
+            send_to(other, mine(near), mine(near), send_sem.at[5], recv_sem.at[8])
+
+    def over_core():
+        far = (x + 2) % 4
+        wait_for(full_ref.at[2 * far, :, :, core], recv_sem.at[6])
+        wait_for(full_ref.at[2 * far + 1, :, :, core], recv_sem.at[7])
+        send_to(other, mine(far), mine(far), send_sem.at[5], recv_sem.at[8])
 
     def finish():
-        wait_for(full_ref.at[:, :, :, core], recv_sem.at[7])
+        wait_for(full_ref.at[:, :, :, core], recv_sem.at[8])
         wait_for(full_ref.at[first, pl.ds(0, 7), y, core], send_sem.at[0])
         wait_for(full_ref.at[second, z, pl.ds(0, 7), core], send_sem.at[1])
         wait_for(full_ref.at[first, :, pl.ds(0, 7), core], send_sem.at[2])
@@ -199,7 +215,7 @@
         wait_for(full_ref.at[pl.ds(0, 6), :, :, core], send_sem.at[4])
         wait_for(full_ref.at[:, :, :, core], send_sem.at[5])
 
-    return [start, lines, over_x, over_core(1), over_core(3), over_core(2), finish]
+    return [start, lines, over_x, forward, over_core, finish]
 
 
 def greet_x(barrier):
@@ -307,12 +323,12 @@
     paced_exchange(
         send,
         receive,
-        [(1, gather[1]), (8, gather[2]), (32, gather[3]), (34, gather[4]), (38, gather[5])],
+        [(1, gather[1]), (7, gather[2]), (19, gather[3]), (28, gather[4])],
     )
     wait_for(send_ref.at[pl.ds(0, LANES - 1)], send_sem)
     for tile in range(FIELDS):
         out_ref[:, tile * LANES : (tile + 1) * LANES] = sums_ref[tile].astype(BF)
-    gather[6]()
+    gather[5]()
 
 
 def window_tile(tile):
@@ -362,6 +378,8 @@
     )
     third_act = third_act.astype(BF).astype(F32)
     last = last_ref[...].astype(F32)
+    last = jnp.concatenate([last[row : row + 1] for row in range(last.shape[0])], axis=1)
+    label = jnp.broadcast_to(label_ref[...].astype(F32), (LANES, LANES)).T[:, :1]
     deep = jnp.sum(third_act * last, axis=1, keepdims=True)
     total = jnp.zeros((feature_ref.shape[0], LANES), F32)
     squares = jnp.zeros((feature_ref.shape[0], LANES), F32)
@@ -370,7 +388,7 @@
         total = total + vector
         squares = squares + vector * vector
     pairs = 0.5 * jnp.sum(total * total - squares, axis=1, keepdims=True)
-    logit_grad = jax.nn.sigmoid(deep + pairs) - label_ref[...].astype(F32)
+    logit_grad = jax.nn.sigmoid(deep + pairs) - label
     h1, h2 = second_ref.shape
     h3 = third_ref.shape[1]
     start = h1 * h2 // LANES
@@ -394,23 +412,30 @@
         )
     after_sums()
     first_grad = (contract(second_grad, second_ref[...], 1, 1) * first_slope).astype(BF)
+    first_grad = first_grad.T
     network_ref[...] = jnp.zeros_like(network_ref)
+    parts = []
+    for z in range(first_ref.shape[1]):
+        weights = [first_ref[block, z].reshape(4 * LANES, LANES) for block in range(blocks)]
+        weights = jnp.concatenate(weights, axis=1)
+        parts.append(jnp.dot(weights, first_grad, preferred_element_type=F32))
+    halves = []
+    for part in parts:
+        upper = part.astype(BF)
+        halves.append((upper, (part - upper.astype(F32)).astype(BF)))
     for tile in range(padded_tiles):
         first, _ = window_tile(tile)
-        z, y = tile // 4, tile % 4 * 2
-        weights = [first_ref[block, z, y : y + 2] for block in range(blocks)]
-        weights = jnp.concatenate([one.reshape(LANES, LANES) for one in weights], axis=1)
-        part = contract(first_grad, weights, 1, 1)
-        upper = part.astype(BF)
-        lower = (part - upper.astype(F32)).astype(BF)
         place = window_map(tile)
-        moved = contract(upper, place, 1, 1) + contract(lower, place, 1, 1)
-        network_ref[first] += moved[:, :LANES]
-        network_ref[first + 1] += moved[:, LANES:]
+        place = jnp.concatenate([place, place], axis=1)
+        rows = slice(tile % 4 * LANES, (tile % 4 + 1) * LANES)
+        pair = jnp.concatenate([half[rows] for half in halves[tile // 4]], axis=0)
+        moved = jnp.dot(place, pair, preferred_element_type=F32)
+        network_ref[first] += moved[:LANES]
+        network_ref[first + 1] += moved[LANES:]
     for tile in range(FIELDS):
         vector = feature_ref[:, tile * LANES : (tile + 1) * LANES].astype(F32)
         grad_ref[tile * LANES : (tile + 1) * LANES] = (
-            network_ref[tile] + logit_grad * (total - vector)
+            network_ref[tile].T + logit_grad * (total - vector)
         ).astype(BF)
 
 
@@ -455,7 +480,7 @@
         for part in range(4):
             mine = packed_ref[pl.ds(pl.multiple_of(core * half + part * eighth, eighth), eighth)]
             theirs = from_core[part * eighth : (part + 1) * eighth]
-            sum_core[part] = (mine + theirs).reshape(sum_core.shape[1:])
+            sum_core[part] = (mine + theirs).reshape(sum_core.shape[1:]).astype(BF)
         for step in range(1, 4):
             to = (x + step) % 4
             send_to(device(x=to), sum_core.at[to], from_x.at[x], send_sem.at[1], recv_sem.at[1])
@@ -464,8 +489,8 @@
     def over_z():
         wait_for(from_x.at[pl.ds(0, 3)], recv_sem.at[1])
         for part in range(8):
-            total = (from_x[0, part] + from_x[1, part]) + (from_x[2, part] + from_x[3, part])
-            sum_x[part] = total.astype(BF)
+            terms = [from_x[one, part].astype(F32) for one in range(4)]
+            sum_x[part] = ((terms[0] + terms[1]) + (terms[2] + terms[3])).astype(BF)
         for step in range(1, 8):
             to = (z + step) % 8
             send_to(device(z=to), sum_x.at[to], from_z.at[z], send_sem.at[2], recv_sem.at[2])
@@ -570,11 +595,11 @@
         receive,
         [
             (2, reduce[1]),
-            (10, reduce[2]),
-            (16, reduce[3]),
-            (21, reduce[4]),
-            (26, reduce[5]),
-            (34, reduce[6]),
+            (9, reduce[2]),
+            (14, reduce[3]),
+            (19, reduce[4]),
+            (24, reduce[5]),
+            (32, reduce[6]),
         ],
     )
     reduce[7]()
@@ -583,7 +608,7 @@
 
 def remote_params(collective_id):
     return pltpu.CompilerParams(
-        vmem_limit_bytes=56 << 20, collective_id=collective_id, has_side_effects=True
+        vmem_limit_bytes=46 << 20, collective_id=collective_id, has_side_effects=True
     )
 
 
@@ -645,13 +670,13 @@
             pltpu.SemaphoreType.DMA,
             pltpu.SemaphoreType.DMA((STEPS,)),
             pltpu.SemaphoreType.DMA((6,)),
-            pltpu.SemaphoreType.DMA((8,)),
+            pltpu.SemaphoreType.DMA((9,)),
             pltpu.VMEM((2, 4, 8) + part, BF),
             pltpu.VMEM((32 * GRAD_ROWS, LANES), F32),
-            pltpu.VMEM((4, 8) + part, F32),
+            pltpu.VMEM((4, 8) + part, BF),
             pltpu.VMEM((8,) + part, BF),
             pltpu.VMEM((8,) + part, BF),
-            pltpu.VMEM((4, 8) + part, F32),
+            pltpu.VMEM((4, 8) + part, BF),
             pltpu.VMEM((8,) + part, BF),
             pltpu.VMEM(part, BF),
             pltpu.SemaphoreType.DMA((7,)),
@@ -661,15 +686,15 @@
         cost_estimate=cost(4 * shards * CAP * FIELDS * samples * width, 400_000_000),
     )(
         piece_dest.reshape(1, pieces),
-        piece_target.reshape(1, pieces),
-        piece_counts.reshape(1, pieces),
+        piece_target.reshape(pieces // LANES, LANES),
+        piece_counts.reshape(pieces // LANES, LANES),
         piece_ids.T,
         table_rows,
         shard,
-        labels.reshape(samples, 1),
+        labels.reshape(1, samples),
         w_second,
         w_third,
-        w_out.reshape(1, h3),
+        w_out.reshape(h3 // LANES, LANES),
     )
     return (row_grad, grad_second, grad_third, grad_out[0])
 

time: 220 us -> 211 us (0.959)
  Pallas kernels: 205 us -> 198 us
    pallas_call x1, Pallas kernels: 205 us -> 198 us  [per_device(): pl.pallas_call(step_kernel, out_shape=(jax.ShapeDtypeStruct((touched, wid...]
    reshape x4 -> x0, local copies, waits for them, and re-layouts: 5.3 us -> none  [the longest x1 1.39 us: per_device(): labels.reshape(samples, 1)]
    unnamed x5 -> x21, local copies, waits for them, and re-layouts: 5.6 us -> 10.3 us
where the time goes in v4:
time: 211 us; the launch traced here: 210 us
  Pallas kernels  198 us (94%)
  local copies, waits for them, and re-layouts  11.7 us (6%)
    pallas_call x1, Pallas kernels, per_device(): pl.pallas_call(step_kernel, out_shape=(jax.ShapeDtypeStruct((touched, wid...  198 us
    unnamed x21, local copies, waits for them, and re-layouts  10.3 us

profile of v4, /device:TPU:1, one launch (start us, length us, event | category | flops | bytes accessed | tf_op | source)
XLA Modules:
  0.0 210.2 jit_solution(2401122906173415759)
XLA Ops:
  0.6 0.9 bitcast_bitcast_fusion.shard_ref
  1.5 0.0 copy-start
  1.5 1.2 copy-done
  2.7 0.0 copy-start.1
  2.7 0.9 copy-done.1
  3.7 0.0 copy-start.2
  3.7 0.9 copy-done.2
  4.6 0.0 copy-start.3
  4.6 0.9 copy-done.3
  5.5 0.0 copy-start.4
  5.5 0.7 copy-done.4
  6.2 0.0 copy-start.5
  6.2 0.7 copy-done.5
  6.9 0.0 copy-start.6
  6.9 0.7 copy-done.6
  7.6 0.0 copy-start.7
  7.6 0.7 copy-done.7
  8.3 0.0 copy-start.8
  8.3 0.7 copy-done.8
  9.0 197.8 %shard_map.129 = (f32[512,128]{1,0:T(8,128)S(1)}, f32[1024,512]{1,0:T(8,128)S(1)}, f32[512,256]{1,0:T(8,128)S(1)}, f32[16,256]{1,0:T(8,128)S(1)}) custom-call(s32[1,4992]{1,0:T(1,128)S(1)} %bitcast.17, s32[39,128]{1,0:T(8,128)S(1)} %bitcast.15, s32[39,128]{1,0:T(8,128)S(1)} %bitcast.16, s32[4,4992]{1,0:T(4,128)S(1)} %bitcast.14, ...), custom_call_target="tpu_custom_call" | custom-call | flops 17448304640 | bytes 400000000 | tf_op jit(solution)/shard_map/pallas_call | solution.py:646
  206.8 0.6 slice.3
  207.4 0.7 copy.20
  208.1 1.3 copy.21
  209.4 0.8 copy.22
Async XLA Ops:
  1.5 1.2 copy-start
  2.7 0.9 copy-start.1
  3.7 0.9 copy-start.2
  4.6 0.9 copy-start.3
  5.5 0.7 copy-start.4
  6.2 0.7 copy-start.5
  6.9 0.7 copy-start.6
  7.6 0.7 copy-start.7
  8.3 0.7 copy-start.8
